TPU v7x, 512 devices: a whole 4x8x8 slice. The times are simulated.
512 devices in a mesh: front: 8 (over y), row: 8 (over x, core), col: 8 (over z).
Axes of the slice: x: 4, y: 8, z: 8, core: 2. Of those that a mesh axis runs over, the one named last changes fastest.
Arguments:
- front_cols: bfloat16 [65536, 256], P(('front', 'row'), 'col'), parts along dimension 0, as said below
- contrib: bfloat16 [64, 3072, 1536], P(('front', 'col'), 'row'), parts along dimension 0, as said below
- child_blocks: int32 [32, 24], P('front'), parts along dimension 0, may hold values from 0 to 63, as said below
- child_live: int32 [32], P('front'), parts along dimension 0, may hold values from 12 to 24
- finish: int32 [64], P('front'), parts along dimension 0, may hold values from 0 to 7, as said below
Outputs:
- schur: bfloat16 [65536, 8192], P(('front', 'row'), 'col'), parts along dimension 0
There are 8 independent parts, one for each index of `front`. A program takes and returns all parts, laid end to end along the dimension named above; each array names one. Nothing has to cross between parts.
Inputs may be any that keep to these rules, and one draw needn't show every extreme that they name: `child_blocks`: row c holds distinct front blocks. With L the row sorted increasingly, entry q equals L[(q % 3) * 8 + 2 * (r % 4) + r // 4] where r = q // 3. At most 4 entries of a row lie in any aligned group of 8 consecutive block numbers, and exactly 4 in some group. `finish`: each value appears once. `contrib`: for each child c, the two pieces that finish names for c, left half then right half, form a symmetric positive definite matrix. `front_cols`: its leading 256 rows form a symmetric positive definite matrix.
All inputs are finite; a program needn't handle non-finite values.
Results may differ from a plain program's by a relative error of at most 0.008.
Values may be sent and summed in bfloat16 or wider, within the bound.
A program may use at most 64 MiB of HBM per device.

v0:
```python
import jax
import jax.numpy as jnp
from jax import lax
from jax.sharding import PartitionSpec as P

PANEL = 256
BLK = 128


def from_everyone(x, axis):
    size = lax.axis_size(axis)
    return lax.all_to_all(jnp.broadcast_to(x[None], (size, *x.shape)), axis, 0, 0, tiled=True)


def laid_out(tiles, dim):
    tiles = jnp.moveaxis(tiles, 0, dim)
    lengths = tiles.shape
    return tiles.reshape(*lengths[:dim], lengths[dim] * lengths[dim + 1], *lengths[dim + 2 :])


def gather_directly(x, axis, dim):
    tiles = from_everyone(x, axis)
    return laid_out(tiles, dim)


def picked_2(x, axis, root):
    return lax.dynamic_index_in_dim(lax.all_gather(x, axis), root, 0, keepdims=False)


def as_sent(x):

    def short(part):
        return part.astype(jnp.bfloat16) if part.dtype == jnp.float32 else part

    return jax.tree.map(short, x)


def one_hot(values, count):
    return values[..., None] == jnp.arange(count, dtype=jnp.int32)


def rank_within(owners):
    count = owners.shape[-1]
    places = jnp.arange(count, dtype=jnp.int32)
    same_owner = owners[..., :, None] == owners[..., None, :]
    earlier = places[None, :] < places[:, None]
    return jnp.sum(same_owner & earlier, axis=-1)


def body(front_cols, contrib, child_blocks, child_live, finish):
    row_count = lax.axis_size("row")
    col_count = lax.axis_size("col")
    own_row = lax.axis_index("row")
    own_col = lax.axis_index("col")
    local_size = front_cols.shape[0]
    group_size = local_size // BLK
    own_piece = contrib[0]
    piece_rows = own_piece.shape[0]
    piece_cols = own_piece.shape[1]
    row_blocks = piece_rows // BLK
    col_blocks = piece_cols // BLK
    spread = row_blocks + 1
    row_cap = min(row_blocks, -(-spread // row_count))
    col_cap = min(col_blocks, -(-spread // 2))
    children = child_blocks.shape[0]
    piece_child = finish // 2
    halves = finish % 2
    picked = one_hot(piece_child, children)
    column_maps = jnp.sum(jnp.where(picked[:, :, None], child_blocks[None, :, :], 0), axis=1)
    column_live = jnp.sum(jnp.where(picked, child_live[None, :], 0), axis=1)
    row_maps = column_maps.reshape(col_count, row_count, row_blocks)
    split_maps = column_maps.reshape(col_count, 2, col_blocks)
    col_maps = jnp.where(halves[:, None] == 0, split_maps[:, 0], split_maps[:, 1])
    row_owner = row_maps // group_size
    row_rank = rank_within(row_owner)
    col_owner = col_maps // group_size
    col_rank = rank_within(col_owner)
    live_rows = column_live[own_col] * BLK
    child_row = own_row * piece_rows + jnp.arange(piece_rows, dtype=jnp.int32)
    child_col = halves[own_col] * piece_cols + jnp.arange(piece_cols, dtype=jnp.int32)
    keep_mask = (
        (child_row[:, None] < live_rows)
        & (child_col[None, :] < live_rows)
        & (child_row[:, None] >= child_col[None, :])
    )
    masked = jnp.where(keep_mask, own_piece, jnp.zeros((), own_piece.dtype))
    sent_row_owner = row_owner[own_col, own_row]
    sent_row_rank = row_rank[own_col, own_row]
    sent_col_owner = col_owner[own_col]
    sent_col_rank = col_rank[own_col]
    col_select = jnp.sum(
        (col_owner == own_col)[:, :, None, None]
        & one_hot(col_rank, col_cap)[:, :, :, None]
        & one_hot(col_maps - own_col * group_size, group_size)[:, :, None, :],
        axis=1,
    ).astype(jnp.bfloat16)
    full_owner = column_maps // group_size
    group_rank = rank_within(full_owner)
    route_rows = one_hot(sent_row_owner * row_cap + sent_row_rank, row_count * row_cap).astype(
        jnp.bfloat16
    )
    outgoing = jnp.einsum(
        "iu,iah->uah",
        route_rows,
        masked.reshape(row_blocks, BLK, piece_cols),
        preferred_element_type=jnp.float32,
    )
    outgoing = outgoing.astype(jnp.bfloat16).reshape(row_count, row_cap, BLK, piece_cols)
    incoming = lax.all_to_all(outgoing, "row", split_axis=0, concat_axis=0, tiled=True)
    mine_owner = full_owner[own_col].reshape(row_count, row_blocks)
    mine_group = group_rank[own_col].reshape(row_count, row_blocks)
    first_select = jnp.sum(
        (mine_owner == own_row)[:, :, None, None]
        & one_hot(row_rank[own_col], row_cap)[:, :, :, None]
        & one_hot(mine_group, spread)[:, :, None, :],
        axis=1,
    ).astype(jnp.bfloat16)
    gathered_rows = jnp.einsum(
        "xsg,xsah->gah", first_select, incoming, preferred_element_type=jnp.float32
    ).astype(jnp.bfloat16)
    route_cols = one_hot(sent_col_owner * col_cap + sent_col_rank, col_count * col_cap).astype(
        jnp.bfloat16
    )
    outgoing = jnp.einsum(
        "ju,gajb->ugab",
        route_cols,
        gathered_rows.reshape(spread, BLK, col_blocks, BLK),
        preferred_element_type=jnp.float32,
    )
    outgoing = outgoing.astype(jnp.bfloat16).reshape(col_count, col_cap, spread, BLK, BLK)
    incoming = lax.all_to_all(outgoing, "col", split_axis=0, concat_axis=0, tiled=True)
    second_select = jnp.sum(
        (full_owner == own_row)[:, :, None, None]
        & one_hot(group_rank, spread)[:, :, :, None]
        & one_hot(column_maps - own_row * group_size, group_size)[:, :, None, :],
        axis=1,
    ).astype(jnp.bfloat16)
    weight = col_select[:, :, None, None, :] * second_select[:, None, :, :, None]
    assembled = jnp.einsum(
        "xsgpq,xsgab->paqb", weight, incoming, preferred_element_type=jnp.float32
    )
    assembled = assembled.reshape(local_size, local_size)
    initial = gather_directly(front_cols, "col", 1).astype(jnp.float32)
    initial = jnp.where(own_col == 0, initial, 0.0)
    assembled = assembled.at[:, :PANEL].add(initial)
    row_ids = own_row * local_size + jnp.arange(local_size, dtype=jnp.int32)
    col_ids = own_col * local_size + jnp.arange(local_size, dtype=jnp.int32)
    lower_part = row_ids[:, None] >= col_ids[None, :]
    assembled = jnp.where(lower_part, assembled, 0.0)
    leading = assembled[:, :PANEL]
    corner = picked_2(leading[:PANEL].astype(jnp.bfloat16), "row", 0).astype(jnp.float32)
    corner = corner + jnp.tril(corner, -1).T
    corner = jnp.where(own_col == 0, corner, jnp.eye(PANEL, dtype=jnp.float32))
    factor = jnp.linalg.cholesky(corner)
    solved = lax.linalg.triangular_solve(
        factor, leading, left_side=False, lower=True, transpose_a=True
    )
    row_panel = picked_2(as_sent(solved), "col", 0).astype(solved.dtype)
    col_panel = picked_2(as_sent(row_panel), "row", own_col).astype(row_panel.dtype)
    update = jnp.einsum(
        "ik,jk->ij",
        row_panel,
        col_panel,
        precision=lax.Precision.HIGHEST,
        preferred_element_type=jnp.float32,
    )
    keep_out = lower_part & (row_ids[:, None] >= PANEL) & (col_ids[None, :] >= PANEL)
    return jnp.where(keep_out, assembled - update, 0.0).astype(jnp.bfloat16)


def solution(mesh):
    return jax.shard_map(
        body,
        mesh=mesh,
        in_specs=(
            P(("front", "row"), "col"),
            P(("front", "col"), "row", None),
            P("front", None),
            P("front"),
            P("front"),
        ),
        out_specs=P(("front", "row"), "col"),
        check_vma=False,
    )
```

profile of v0, /device:TPU:1, one launch (start us, length us, event | category | flops | bytes accessed | tf_op | source)
XLA Modules:
  0.0 356.3 jit_solution(16613479188600580803)
XLA Ops:
  12.6 3.8 %fusion.1 = bf16[8,1,128,1536]{3,0,2,1:T(8,128)(2,1)S(1)} fusion(bf16[3,128,1536]{2,1,0:T(8,128)(2,1)} %bitcast.104, s32[1536]{0:T(1024)S(1)} %iota_add_fusion, s32[3,128]{0,1:T(8,128)S(1)} %add_add_fusion, pred[1536]{0:T(1024)(128)(4,1)S(1)} %broadcast_compare_fusion.1, pred[3,128]{0,1:T(8,128)(4,1)S(1)} %broadcast_compare_fusion, s32[3]{0:T(128)S(1)} %fusion.48), kind=kOutput, calls=%fused_computation.8 | convolution fusion | flops 13369368 | bytes 4334988 | tf_op jit(solution)/shard_map/iu,iah->uah/dot_general | solution.py:102
  16.4 2.6 copy.134
  19.0 10.6 %all-to-all-start = ((bf16[8,1,128,1536]{3,2,1,0:T(8,128)(2,1)}), bf16[8,1,128,1536]{3,2,1,0:T(8,128)(2,1)S(1)}, u32[]{:S(2)}, u32[]{:S(2)}) async-start(bf16[8,1,128,1536]{3,2,1,0:T(8,128)(2,1)} %copy.134), calls=%async_computation | async-start | bytes 6291456 | tf_op jit(solution)/shard_map/all_to_all | solution.py:109
  30.5 36.6 %all-to-all-done = bf16[8,1,128,1536]{3,2,1,0:T(8,128)(2,1)S(1)} async-done(((bf16[8,1,128,1536]{3,2,1,0:T(8,128)(2,1)}), bf16[8,1,128,1536]{3,2,1,0:T(8,128)(2,1)S(1)}, u32[]{:S(2)}, u32[]{:S(2)}) %all-to-all-start) | async-done | bytes 3145760 | tf_op jit(solution)/shard_map/all_to_all | solution.py:109
  68.0 5.4 %all-to-all-start.2 = ((bf16[8,1024,32]{1,2,0:T(8,128)(2,1)}), bf16[8,1024,32]{1,2,0:T(8,128)(2,1)}, u32[]{:S(2)}, u32[]{:S(2)}) async-start(bf16[8,1024,32]{1,2,0:T(8,128)(2,1)} %broadcast_in_dim.67), calls=%async_computation.2 | async-start | bytes 1048576 | tf_op jit(solution)/shard_map/all_to_all | solution.py:12
  74.0 3.3 fusion.5
  77.2 3.9 %copy.136 = bf16[4,128,1536]{1,2,0:T(8,128)(2,1)} copy(bf16[4,128,1536]{2,0,1:T(4,128)(2,1)} %fusion.5) | data formatting | bytes 3145728 | tf_op jit(solution)/shard_map/convert_element_type | solution.py:120
  81.1 3.3 copy.137
  85.1 2.9 copy.138
  88.1 3.0 all-to-all-done.2
  91.0 4.3 %all-to-all-start.1 = ((bf16[8,2,4,128,128]{4,1,2,3,0:T(2,128)(2,1)}), bf16[8,2,4,128,128]{4,1,2,3,0:T(2,128)(2,1)}, u32[]{:S(2)}, u32[]{:S(2)}) async-start(bf16[8,2,4,128,128]{4,1,2,3,0:T(2,128)(2,1)} %copy.138), calls=%async_computation.1 | async-start | bytes 4194304 | tf_op jit(solution)/shard_map/all_to_all | solution.py:131
  97.7 1.1 convert_select_fusion
  99.2 44.6 %all-to-all-done.1 = bf16[8,2,4,128,128]{4,1,2,3,0:T(2,128)(2,1)} async-done(((bf16[8,2,4,128,128]{4,1,2,3,0:T(2,128)(2,1)}), bf16[8,2,4,128,128]{4,1,2,3,0:T(2,128)(2,1)}, u32[]{:S(2)}, u32[]{:S(2)}) %all-to-all-start.1) | async-done | bytes 2097184 | tf_op jit(solution)/shard_map/all_to_all | solution.py:131
  143.7 3.2 convolution_bitcast_fusion
  148.3 1.1 fusion.15
  149.7 1.6 copy-done
  151.2 2.0 copy-done.1
  154.0 26.9 %all-gather.9.cloned.1.call-done = bf16[2048,256]{1,0:T(8,128)(2,1)} async-done(((bf16[256,256]{1,0:T(8,128)(2,1)}), bf16[2048,256]{1,0:T(8,128)(2,1)}) %all-gather.9.cloned.1.call-update) | async-done | bytes 1048592 | tf_op jit(solution)/shard_map/all_gather | solution.py:27
  181.9 1.0 fusion.23
  183.2 11.7 %cholesky.49 = f32[128,128]{1,0:T(8,128)S(1)} custom-call(f32[128,128]{1,0:T(8,128)S(1)} %cholesky.115), custom_call_target="Cholesky" | custom-call | tf_op jit(solution)/shard_map/jit(cholesky)/cholesky | solution.py:154
  195.6 9.8 %custom-call.14 = f32[1,128,128]{1,2,0:T(8,128)S(1)} custom-call(f32[1,128,128]{2,1,0:T(8,128)S(1)} %get-tuple-element.44), custom_call_target="InvertDiagBlocksLowerTriangular" | custom-call | tf_op jit(solution)/shard_map/jit(cholesky)/cholesky | solution.py:154
  205.9 11.7 %cholesky.103 = f32[128,128]{1,0:T(8,128)S(1)} custom-call(f32[128,128]{1,0:T(8,128)S(1)} %convolution_subtract_fusion.1), custom_call_target="Cholesky" | custom-call | tf_op jit(solution)/shard_map/jit(cholesky)/cholesky | solution.py:154
  219.6 4.0 %while.2 = (s32[]{:T(128)}, f32[256,256]{1,0:T(8,128)S(1)}, s32[2,2]{1,0:T(2,128)S(1)}, f32[2,128,128]{2,1,0:T(8,128)S(1)}, s32[]{:T(128)}) while((s32[]{:T(128)}, f32[256,256]{1,0:T(8,128)S(1)}, s32[2,2]{1,0:T(2,128)S(1)}, f32[2,128,128]{2,1,0:T(8,128)S(1)}, s32[]{:T(128)}) %tuple.33), condition=%wide.while_cond.1, body=%wide.while_body.1.sunk | while | flops 2 | bytes 131189 | solution.py:155
  220.3 1.3 bitcast_dynamic-update-slice_fusion.2
  222.3 1.3 bitcast_dynamic-update-slice_fusion.2
  223.6 19.7 %custom-call.15 = f32[2,128,128]{1,2,0:T(8,128)S(1)} custom-call(f32[2,128,128]{2,1,0:T(8,128)S(1)} %get-tuple-element.24), custom_call_target="InvertDiagBlocksLowerTriangular" | custom-call | tf_op jit(solution)/shard_map/triangular_solve | solution.py:155
  243.3 1.7 fusion.17
  244.9 2.0 convolution_subtract_fusion
  248.8 57.7 %all-gather.5.cloned.1.call-done = bf16[8,1024,256]{2,1,0:T(8,128)(2,1)} async-done(((bf16[1,1024,256]{2,1,0:T(8,128)(2,1)}), bf16[8,1024,256]{2,1,0:T(8,128)(2,1)}) %all-gather.5.cloned.1.call-update) | async-done | bytes 4194320 | tf_op jit(solution)/shard_map/all_gather | solution.py:27
  306.5 1.9 dynamic_slice.51
  308.4 36.2 %all-gather.7.cloned.1.call-done = bf16[8,1024,256]{2,1,0:T(8,128)(2,1)} async-done(((bf16[1,1024,256]{2,1,0:T(8,128)(2,1)}), bf16[8,1024,256]{2,1,0:T(8,128)(2,1)}) %all-gather.7.cloned.1.call-update) | async-done | bytes 4194320 | tf_op jit(solution)/shard_map/all_gather | solution.py:27
  344.6 5.2 %select_convert_fusion = bf16[1024,1024]{1,0:T(8,128)(2,1)} fusion(s32[1024]{0:T(1024)S(1)} %get-tuple-element.50, s32[1024]{0:T(1024)S(1)} %get-tuple-element.51, pred[1024]{0:T(1024)(128)(4,1)S(1)} %get-tuple-element.53, pred[1024]{0:T(1024)(128)(4,1)S(1)} %get-tuple-element.52, bf16[8,1024,256]{2,1,0:T(8,128)(2,1)} %all-gather.7.cloned.1.call-done, ...), kind=kOutput, calls=%fused_computation.5 | convolution fusion | flops 544210944 | bytes 7350276 | tf_op jit(solution)/shard_map/ik,jk->ij/dot_general | solution.py:160
  (94 shorter events, 18.8 us)
Async XLA Ops:
  19.0 48.2 %copy-start.2 = (bf16[1024,32]{0,1:T(8,128)(2,1)S(1)}, bf16[1024,32]{0,1:T(8,128)(2,1)}, u32[]{:S(2)}) copy-start(bf16[1024,32]{0,1:T(8,128)(2,1)} %param.7) | copy-start | bytes 196612
  19.0 48.1 %all-to-all-start = ((bf16[8,1,128,1536]{3,2,1,0:T(8,128)(2,1)}), bf16[8,1,128,1536]{3,2,1,0:T(8,128)(2,1)S(1)}, u32[]{:S(2)}, u32[]{:S(2)}) async-start(bf16[8,1,128,1536]{3,2,1,0:T(8,128)(2,1)} %copy.134), calls=%async_computation | async-start | bytes 6291456 | tf_op jit(solution)/shard_map/all_to_all | solution.py:109
  68.0 23.1 %all-to-all-start.2 = ((bf16[8,1024,32]{1,2,0:T(8,128)(2,1)}), bf16[8,1024,32]{1,2,0:T(8,128)(2,1)}, u32[]{:S(2)}, u32[]{:S(2)}) async-start(bf16[8,1024,32]{1,2,0:T(8,128)(2,1)} %broadcast_in_dim.67), calls=%async_computation.2 | async-start | bytes 1048576 | tf_op jit(solution)/shard_map/all_to_all | solution.py:12
  91.0 52.7 %all-to-all-start.1 = ((bf16[8,2,4,128,128]{4,1,2,3,0:T(2,128)(2,1)}), bf16[8,2,4,128,128]{4,1,2,3,0:T(2,128)(2,1)}, u32[]{:S(2)}, u32[]{:S(2)}) async-start(bf16[8,2,4,128,128]{4,1,2,3,0:T(2,128)(2,1)} %copy.138), calls=%async_computation.1 | async-start | bytes 4194304 | tf_op jit(solution)/shard_map/all_to_all | solution.py:131
  95.4 85.5 %all-gather.9.cloned.1.call-start = ((), (), s32[]{:S(2)}) async-start(), calls=%async_computation.5 | async-start | bytes 1179648 | tf_op jit(solution)/shard_map/all_gather | solution.py:27
  149.3 1.9 copy-start
  151.2 2.0 copy-start.1
  153.9 152.6 %all-gather.5.cloned.1.call-start = ((), (), s32[]{:S(2)}) async-start(), calls=%async_computation.3 | async-start | bytes 4718592 | tf_op jit(solution)/shard_map/all_gather | solution.py:27
  248.7 95.9 %all-gather.7.cloned.1.call-start = ((), (), s32[]{:S(2)}) async-start(), calls=%async_computation.4 | async-start | bytes 4718592 | tf_op jit(solution)/shard_map/all_gather | solution.py:27
Sparse Core Ops, SparseCore 0:
  154.0 26.8 all-gather.8
  248.8 57.5 all-gather.4
  308.6 35.9 all-gather.6
where the time goes:
time: 357 us; the launch traced here: 356 us
  waiting for transfers between devices  205 us (57%)
  other arithmetic  64.8 us (18%)
  local copies, waits for them, and re-layouts  28.7 us (8%)
  matrix products  20.9 us (6%)
  starting transfers between devices  20.6 us (6%)
  between operations  16.1 us (5%)
    all_gather x3, waiting for transfers between devices, picked_2(): lax.all_gather(x, axis)  121 us
    all_to_all x1, waiting for transfers between devices, body(): lax.all_to_all(outgoing, 'col', split_axis=0, concat_axis=0, tiled=True)  44.6 us
    all_to_all x1, waiting for transfers between devices, body(): lax.all_to_all(outgoing, 'row', split_axis=0, concat_axis=0, tiled=True)  36.6 us
    another operation x7, other arithmetic, body(): factor = jnp.linalg.cholesky(corner)  34.6 us
    another operation x5, other arithmetic, body(): lax.linalg.triangular_solve(factor, leading, left_side=False, lower=True,...  19.8 us
    all_to_all x1, starting transfers between devices, body(): lax.all_to_all(outgoing, 'row', split_axis=0, concat_axis=0, tiled=True)  10.6 us
  transfers between devices with their start and end apart: 6, of which 6 were waited for; matrix products, arithmetic and copies ran while one was open for 5% of the time, Pallas kernels for 0%

commit v1 on v0

v1 whole, which is shorter than its diff:
```python
import jax
import jax.numpy as jnp
from jax import lax
from jax.experimental import pallas as pl
from jax.experimental.pallas import tpu as pltpu
from jax.sharding import PartitionSpec as P

BLK = 128
PANEL = 256
N = 8
CHIPS = 4
BLOCKS = 24
BF16 = jnp.bfloat16
F32 = jnp.float32
LAG = 1


def copy_to(src, dst, send, recv, **device):
    return pltpu.make_async_remote_copy(
        src_ref=src,
        dst_ref=dst,
        send_sem=send,
        recv_sem=recv,
        device_id=device,
        device_id_type=pl.DeviceIdType.MESH,
    )


def ring_offset(i):
    return jnp.where(i % 2 == 1, (i + 1) // 2, (N - i // 2) % N)


def first_kept(col):
    return jnp.where(col < 4, 0, jnp.where(col < 6, 1, 2))


def chosen(cases):
    value = cases[0][1]
    for holds, other in cases[1:]:
        value = jnp.where(holds, other, value)
    return value


def column_block(m):
    place = 3 * (m % 4) + m // 4
    return slice(place * BLK, (place + 1) * BLK)


def exchange_kernel(
    cb, live, fin, contrib, fcp,
    xr_o, pr_o, pc_o, co_o,
    px, pxr, pz, pzr, pb, pr, pt, pc, co, zs, zr, xs, xr,
    px_s, px_r, pz_s, pz_r, pr_s, pr_r, t_s, t_r, pc_s, pc_r, co_s, co_r,
    z_s, z_r, x_s, x_r, f_s, f_r, o_s,
):
    row = lax.axis_index("row")
    col = lax.axis_index("col")
    chip = row // 2
    core = row % 2
    mate = 2 * chip + 1 - core

    barrier = pltpu.get_barrier_semaphore()

    @pl.loop(1, N)
    def _(d):
        pl.semaphore_signal(barrier, 1, device_id={"row": (row + d) % N}, device_id_type=pl.DeviceIdType.MESH)
        pl.semaphore_signal(barrier, 1, device_id={"col": (col + d) % N}, device_id_type=pl.DeviceIdType.MESH)

    @pl.when(row != col)
    def _():
        pl.semaphore_signal(barrier, 1, device_id={"row": col, "col": row}, device_id_type=pl.DeviceIdType.MESH)

    piece = fin[col]
    child = piece >> 1
    half = piece & 1
    groups = [cb[child, 3 * row + k] >> 3 for k in range(3)]
    for dest in range(N):
        px[dest] = chosen([(groups[k] == dest, contrib[k, :, 0:BLK]) for k in range(3)])
    pxr[row] = px[row]

    @pl.when(row == col)
    def _():
        pl.semaphore_wait(barrier, 2 * N - 2)

    @pl.when(row != col)
    def _():
        pl.semaphore_wait(barrier, 2 * N - 1)

    def px_copy(dest, slot):
        return copy_to(px.at[dest], pxr.at[slot], px_s.at[dest], px_r.at[slot], row=dest)

    @pl.loop(1, N)
    def _(d):
        dest = (row + d) % N
        px_copy(dest, row).start()

    col_groups = [cb[child, 12 * half + 3 * (m % 4) + m // 4] >> 3 for m in range(12)]
    for dest in range(N):
        first = sum(jnp.where(g < dest, 1, 0) for g in col_groups)
        for k in range(0 if dest < 4 else 1 if dest < 6 else 2, 3):
            for c in range(2):
                ms = range(max(0, 2 * dest - 4 + c), min(2 * dest + 1, 4 * k + 3) + 1)
                zs[dest, k, c] = chosen([(first == m - c, contrib[k, :, column_block(m)]) for m in ms])
    zr[col] = zs[col]

    from_row = [jnp.int32(0)] * N
    for q in range(BLOCKS):
        at = cb[child, q] - N * row
        from_row = [jnp.where(at == b, q // 3, from_row[b]) for b in range(N)]

    @pl.loop(1, N)
    def _(d):
        px_copy((row + d) % N, (row + d) % N).wait_recv()

    for b in range(N):
        pz[b, 0:BLK] = chosen([(from_row[b] == r, pxr[r]) for r in range(N)])
        pz[b, BLK:] = fcp[b]
    pzr[col] = pz[col]

    def pz_copy(dest, slot):
        return copy_to(pz.at[dest], pzr.at[slot], pz_s.at[dest], pz_r.at[slot], col=dest)

    @pl.loop(1, N)
    def _(i):
        dest = (col + ring_offset(i)) % N
        pz_copy(dest, col).start()

    def z_copies(dest, slot, by, act):
        for k in range(3):
            @pl.when(first_kept(by) == k)
            def _():
                act(copy_to(
                    zs.at[dest, pl.ds(k, 3 - k)], zr.at[slot, pl.ds(k, 3 - k)],
                    z_s.at[dest], z_r.at[slot], col=dest,
                ))

    @pl.loop(1, N)
    def _(i):
        dest = (col + ring_offset(i)) % N
        z_copies(dest, col, dest, lambda copy: copy.start())

    @pl.loop(1, N)
    def _(i):
        pz_copy((col + i) % N, (col + i) % N).wait_recv()

    left = jnp.zeros((BLK, BLK), F32)
    right = jnp.zeros((BLK, BLK), F32)
    for j in range(N):
        c = fin[j] >> 1
        column = 12 * (fin[j] & 1)
        q = jnp.int32(-1)
        for a in range(BLOCKS):
            q = jnp.where(cb[c, a] == N * row + col, a, q)
        at = cb[c, column]
        valid = (q >= column) & (q < live[c])
        block = pzr[j, 0:BLK].astype(F32)
        left += jnp.where(valid & (at == 0), block, 0.0)
        right += jnp.where(valid & (at == 1), block, 0.0)
    lane = lax.broadcasted_iota(jnp.int32, (32, BLK), 1) // 32
    packed = [pzr[j, BLK:].astype(F32) for j in range(N)]
    for s in range(4):
        parts = []
        for side in range(2):
            part = jnp.zeros((32, BLK), F32)
            for j in range(4):
                moved = packed[4 * side + j]
                if (j - s) % 4:
                    moved = pltpu.roll(moved, 32 * ((j - s) % 4), 1)
                part = jnp.where(lane == j, moved, part)
            parts.append(part)
        rows = slice(32 * s, 32 * s + 32)
        row_ids = (N * row + col) * BLK + 32 * s + lax.broadcasted_iota(jnp.int32, (32, BLK), 0)
        col_ids = lax.broadcasted_iota(jnp.int32, (32, BLK), 1)
        pb[rows, 0:BLK] = jnp.where(row_ids >= col_ids, left[rows] + parts[0], 0.0).astype(BF16)
        pb[rows, BLK:] = jnp.where(row_ids >= col_ids + BLK, right[rows] + parts[1], 0.0).astype(BF16)
    pr[col] = pb[...]

    def pr_copy(dest, slot):
        return copy_to(pb, pr.at[slot], pr_s.at[dest], pr_r.at[slot], col=dest)

    pt_copy = copy_to(pb, pt, t_s, t_r, row=col, col=row)

    @pl.when(row != col)
    def _():
        pt_copy.start()

    @pl.loop(1, N)
    def _(i):
        dest = (col + ring_offset(i)) % N

        @pl.when((dest <= row) | (row == 0))
        def _():
            pr_copy(dest, col).start()

    @pl.when(row == col)
    def _():
        pt[...] = pb[...]

    @pl.when(row != col)
    def _():
        pt_copy.wait_recv()

    def pc_copy(dest, slot):
        return copy_to(pt, pc.at[slot], pc_s.at[dest], pc_r.at[slot], row=dest)

    @pl.loop(1, N)
    def _(i):
        dest = (row + i) % N

        @pl.when(dest >= col)
        def _():
            pc_copy(dest, row).start()

    pc[row] = pt[...]

    def co_copy(dest):
        return copy_to(pr.at[pl.ds(0, 2)], co, co_s.at[dest], co_r, row=dest)

    @pl.when(row == 0)
    def _():
        for b in range(2):
            @pl.when(col != b)
            def _():
                pr_copy(b, b).wait_recv()

        @pl.loop(1, N)
        def _(dest):
            co_copy(dest).start()

        co[...] = pr[0:2]

    needed = chip >= col // 2

    def x_copy(j, src, dest, slot):
        return copy_to(src, xr.at[core, j, slot], x_s.at[j, dest], x_r.at[j, slot], row=2 * dest + core)

    def f_copy(j, side):
        return copy_to(xr.at[side, j], xr.at[side, j], f_s.at[j], f_r.at[j], row=mate)

    @pl.loop(0, N + LAG)
    def _(i):
        j = (col + ring_offset(i)) % N

        @pl.when(i < N)
        def _():
            @pl.when(i > 0)
            def _():
                z_copies(j, j, col, lambda copy: copy.wait_recv())

            c = fin[j] >> 1
            for dest in range(CHIPS):
                @pl.when(2 * dest + 1 >= col)
                def _():
                    if dest == 0:
                        src = zr.at[j, 0]
                    elif dest == 3:
                        src = zr.at[j, 2]
                    else:
                        src = xs.at[j, dest - 1]
                        later = (cb[c, 3 * row + dest] >> 4) == dest
                        src[...] = jnp.where(later, zr[j, dest], zr[j, dest - 1])

                    @pl.when(chip == dest)
                    def _():
                        xr[core, j, chip] = src[...]

                    @pl.when(chip != dest)
                    def _():
                        x_copy(j, src, dest, chip).start()

        @pl.when((i >= LAG) & needed)
        def _():
            before = (col + ring_offset(i - LAG)) % N
            for slot in range(CHIPS):
                @pl.when(chip != slot)
                def _():
                    x_copy(before, xs.at[before, 0], slot, slot).wait_recv()

            f_copy(before, core).start()

    @pl.when(row != 0)
    def _():
        co_copy(row).wait_recv()

    @pl.loop(1, N)
    def _(i):
        b = (col + i) % N

        @pl.when(((row == 0) & (b > 1)) | ((row > 0) & (col <= row)))
        def _():
            pr_copy(b, b).wait_recv()

        @pl.when(row >= col)
        def _():
            slot = (row + i) % N
            pc_copy(slot, slot).wait_recv()

    out_co = pltpu.make_async_copy(co, co_o, o_s.at[0])
    out_pr = pltpu.make_async_copy(pr, pr_o, o_s.at[1])
    out_pc = pltpu.make_async_copy(pc, pc_o, o_s.at[2])
    out_xr = pltpu.make_async_copy(xr, xr_o, o_s.at[3])
    out_co.start()

    @pl.when(row >= col)
    def _():
        out_pr.start()
        out_pc.start()

    @pl.when(needed)
    def _():
        @pl.loop(0, N)
        def _(j):
            f_copy(j, 1 - core).wait_recv()

    @pl.when(row >= col)
    def _():
        out_xr.start()
        out_xr.wait()
        out_pr.wait()
        out_pc.wait()

    out_co.wait()

    @pl.loop(1, N)
    def _(i):
        r = (row + i) % N
        c = (col + i) % N
        px_copy(r, row).wait_send()
        pz_copy(c, col).wait_send()
        z_copies(c, col, c, lambda copy: copy.wait_send())

        @pl.when((c <= row) | (row == 0))
        def _():
            pr_copy(c, col).wait_send()

        @pl.when(r >= col)
        def _():
            pc_copy(r, row).wait_send()

        @pl.when(row == 0)
        def _():
            co_copy(r).wait_send()

    @pl.when(row != col)
    def _():
        pt_copy.wait_send()

    @pl.loop(0, N)
    def _(j):
        for dest in range(CHIPS):
            @pl.when((2 * dest + 1 >= col) & (chip != dest))
            def _():
                x_copy(j, xs.at[j, 0], dest, chip).wait_send()

        @pl.when(needed)
        def _():
            f_copy(j, core).wait_send()


def exchange(cb, live, fin, contrib, fcp):
    dma = pltpu.SemaphoreType.DMA
    any_ = pl.BlockSpec(memory_space=pl.ANY)
    vmem = pl.BlockSpec(memory_space=pltpu.VMEM)
    smem = pl.BlockSpec(memory_space=pltpu.SMEM)
    block = (BLK, BLK)
    panel = (BLK, PANEL)
    return pl.pallas_call(
        exchange_kernel,
        out_shape=[
            jax.ShapeDtypeStruct((2, N, CHIPS, 2, *block), BF16),
            jax.ShapeDtypeStruct((N, *panel), BF16),
            jax.ShapeDtypeStruct((N, *panel), BF16),
            jax.ShapeDtypeStruct((2, *panel), BF16),
        ],
        in_specs=[smem, smem, smem, vmem, vmem],
        out_specs=[any_] * 4,
        scratch_shapes=[
            pltpu.VMEM((N, *block), BF16),
            pltpu.VMEM((N, *block), BF16),
            pltpu.VMEM((N, BLK + 32, BLK), BF16),
            pltpu.VMEM((N, BLK + 32, BLK), BF16),
            pltpu.VMEM(panel, BF16),
            pltpu.VMEM((N, *panel), BF16),
            pltpu.VMEM(panel, BF16),
            pltpu.VMEM((N, *panel), BF16),
            pltpu.VMEM((2, *panel), BF16),
            pltpu.VMEM((N, 3, 2, *block), BF16),
            pltpu.VMEM((N, 3, 2, *block), BF16),
            pltpu.VMEM((N, 2, 2, *block), BF16),
            pltpu.VMEM((2, N, CHIPS, 2, *block), BF16),
            dma((N,)), dma((N,)),
            dma((N,)), dma((N,)),
            dma((N,)), dma((N,)),
            dma, dma,
            dma((N,)), dma((N,)),
            dma((N,)), dma,
            dma((N,)), dma((N,)),
            dma((N, CHIPS)), dma((N, CHIPS)),
            dma((N,)), dma((N,)),
            dma((4,)),
        ],
        compiler_params=pltpu.CompilerParams(
            collective_id=0, has_side_effects=True, vmem_limit_bytes=40 << 20
        ),
        name="exchange",
    )(cb, live, fin, contrib, fcp)


def dot(a, b):
    return jnp.dot(a, b, preferred_element_type=F32, precision=lax.Precision.HIGHEST)


def small_inverse(d):
    n = d.shape[0]
    rows = lax.broadcasted_iota(jnp.int32, (n, n), 0)
    cols = lax.broadcasted_iota(jnp.int32, (n, n), 1)
    for k in range(n):
        inv = 1.0 / d[k : k + 1, k : k + 1]
        across = d[k : k + 1, :] * inv
        down = d[:, k : k + 1]
        d = d - down * across
        d = jnp.where(rows == k, across, d)
        d = jnp.where(cols == k, jnp.where(rows == k, -inv, down * inv), d)
    return -d


STEP = 32


def sweep_block(a):
    across = a[0:STEP, :]
    down = a[:, 0:STEP]
    inv = small_inverse(a[0:STEP, 0:STEP])
    q = dot(inv, across)
    qt = dot(down, inv)
    a[...] = a[...] - dot(qt, across)
    a[0:STEP, :] = q
    a[:, 0:STEP] = qt
    a[0:STEP, 0:STEP] = -inv
    n = a.shape[0]
    a[...] = pltpu.roll(pltpu.roll(a[...], n - STEP, 0), n - STEP, 1)


def update_kernel(cb, live, fin, xr, pr, pc, co, out, a, t, total, rowq, colq, colc, jof):
    row = lax.axis_index("row")
    col = lax.axis_index("col")
    p = pl.program_id(0)

    @pl.when((p == 0) & (row >= col))
    def _():
        lower = jnp.concatenate([co[0], co[1]], axis=0).astype(F32)
        ri = lax.broadcasted_iota(jnp.int32, (PANEL, PANEL), 0)
        ci = lax.broadcasted_iota(jnp.int32, (PANEL, PANEL), 1)
        a[...] = lower + jnp.where(ri < ci, lower.T, 0.0)

        @pl.loop(0, PANEL // STEP)
        def _(i):
            sweep_block(a)

        m = -a[...]
        high = m.astype(BF16)
        low = (m - high.astype(F32)).astype(BF16)
        rows = pr[...].reshape(N * BLK, PANEL)
        t[...] = (
            jnp.dot(rows, high, preferred_element_type=F32)
            + jnp.dot(rows, low, preferred_element_type=F32)
        ).astype(BF16)

        for i in range(4 * N):
            rowq[i] = -1
            colq[i] = -1
        for j in range(N):
            jof[fin[j]] = j
        for c in range(4):
            for q in range(BLOCKS):
                v = cb[c, q]
                m = 4 * (q % 3) + (q // 3) % 4
                before = q - q % 12 + 3 * ((m - 1) % 4) + (m - 1) // 4

                @pl.when(v >> 3 == row)
                def _():
                    rowq[N * c + (v & 7)] = q

                @pl.when(v >> 3 == col)
                def _():
                    colq[N * c + (v & 7)] = q
                    if m == 0:
                        colc[N * c + (v & 7)] = 0
                    else:
                        colc[N * c + (v & 7)] = jnp.where(cb[c, before] >> 3 == col, 1, 0)

    @pl.when(row < col)
    def _():
        out[...] = jnp.zeros_like(out)

    @pl.when(row >= col)
    def _():
        rows = t[pl.ds(pl.multiple_of(p * BLK, BLK), BLK), :]
        for b in range(0, N, 2):
            columns = pc[b : b + 2].reshape(2 * BLK, PANEL)
            total[:, b * BLK : (b + 2) * BLK] = -lax.dot_general(
                rows, columns, (((1,), (1,)), ((), ())), preferred_element_type=F32
            )
        for c in range(4):
            q = rowq[N * c + p]

            @pl.when((q >= 0) & (q < live[c]))
            def _():
                r = q // 3
                for b in range(N):
                    s = colq[N * c + b]

                    @pl.when((s >= 0) & (s <= q))
                    def _():
                        j = jof[2 * c + jnp.where(s >= 12, 1, 0)]
                        block = xr[r % 2, j, r // 2, colc[N * c + b]]
                        total[:, b * BLK : (b + 1) * BLK] += block.astype(F32)

        ri = (N * row + p) * BLK + lax.broadcasted_iota(jnp.int32, (BLK, N * BLK), 0)
        ci = N * BLK * col + lax.broadcasted_iota(jnp.int32, (BLK, N * BLK), 1)
        keep = (ri >= ci) & (ri >= PANEL) & (ci >= PANEL)
        out[...] = jnp.where(keep, total[...], 0.0).astype(BF16)


def update(cb, live, fin, xr, pr, pc, co):
    smem = pl.BlockSpec(memory_space=pltpu.SMEM)
    vmem = pl.BlockSpec(memory_space=pltpu.VMEM)
    ints = lambda n: pltpu.SMEM((n,), jnp.int32)
    return pl.pallas_call(
        update_kernel,
        grid=(N,),
        out_shape=jax.ShapeDtypeStruct((N * BLK, N * BLK), BF16),
        in_specs=[smem] * 3 + [vmem] * 4,
        out_specs=pl.BlockSpec((BLK, N * BLK), lambda p: (p, 0)),
        scratch_shapes=[
            pltpu.VMEM((PANEL, PANEL), F32),
            pltpu.VMEM((N * BLK, PANEL), BF16),
            pltpu.VMEM((BLK, N * BLK), F32),
            ints(4 * N), ints(4 * N), ints(4 * N), ints(N),
        ],
        compiler_params=pltpu.CompilerParams(vmem_limit_bytes=40 << 20),
        name="update",
    )(cb, live, fin, xr, pr, pc, co)


def body(front_cols, contrib, child_blocks, child_live, finish):
    packed = front_cols.reshape(N, 4, 32, 32).transpose(0, 2, 1, 3).reshape(N, 32, BLK)
    pieces = contrib.reshape(3, BLK, 12 * BLK)
    xr, pr, pc, co = exchange(child_blocks, child_live, finish, pieces, packed)
    return update(child_blocks, child_live, finish, xr, pr, pc, co)


def solution(mesh):
    return jax.shard_map(
        body,
        mesh=mesh,
        in_specs=(
            P(("front", "row"), "col"),
            P(("front", "col"), "row", None),
            P("front", None),
            P("front"),
            P("front"),
        ),
        out_specs=P(("front", "row"), "col"),
        check_vma=False,
    )
```

time: 357 us -> 150 us (0.42)
  waiting for transfers between devices: 205 us -> 0 us
  Pallas kernels: 0 us -> 145 us
  other arithmetic: 64.8 us -> 0 us
  local copies, waits for them, and re-layouts: 28.7 us -> 4.85 us
  matrix products: 20.9 us -> 0 us
  starting transfers between devices: 20.6 us -> 0 us
  between operations: 16.1 us -> 0.04 us
    pallas_call x0 -> x2, Pallas kernels: none -> 145 us  [the longest x1 99.5 us: exchange(): pl.pallas_call(exchange_kernel, out_shape=[jax.ShapeDtypeStruct((2, N, CH...]
    all_gather x3 -> x0, waiting for transfers between devices: 121 us -> none  [picked_2(): lax.all_gather(x, axis)]
    all_to_all x3 -> x0, waiting for transfers between devices: 84.2 us -> none  [the longest x1 44.6 us: body(): lax.all_to_all(outgoing, 'col', split_axis=0, concat_axis=0, tiled=True)]
    another operation x13 -> x0, other arithmetic: 55 us -> none  [the longest x7 34.6 us: body(): factor = jnp.linalg.cholesky(corner)]
    all_to_all x3 -> x0, starting transfers between devices: 20.3 us -> none  [the longest x1 10.6 us: body(): lax.all_to_all(outgoing, 'row', split_axis=0, concat_axis=0, tiled=True)]
    dot_general x5 -> x0, matrix products: 16.1 us -> none  [the longest x1 5.16 us: body(): jnp.einsum('ik,jk->ij', row_panel, col_panel, precision=lax.Precision.HIG...]
    reshape x6 -> x3, local copies, waits for them, and re-layouts: 9.13 us -> 1.59 us  [body(): front_cols.reshape(N, 4, 32, 32).transpose(0, 2, 1, 3).reshape(N, 32, BLK)]
    another operation x10 -> x0, local copies, waits for them, and re-layouts: 4.89 us -> none
  transfers between devices with their start and end apart: 6 -> 0, of which waited for: 6 -> 0; matrix products, arithmetic and copies ran while one was open for 5% -> 0% of each run, Pallas kernels for 0% -> 0%
where the time goes in v1:
time: 150 us
  Pallas kernels  145 us (97%)
  local copies, waits for them, and re-layouts  4.85 us (3%)
    pallas_call x1, Pallas kernels, exchange(): pl.pallas_call(exchange_kernel, out_shape=[jax.ShapeDtypeStruct((2, N, CH...  99.5 us
    pallas_call x1, Pallas kernels, update(): pl.pallas_call(update_kernel, grid=(N,), out_shape=jax.ShapeDtypeStruct((...  45.8 us
    unnamed x8, local copies, waits for them, and re-layouts  3.26 us

profile of v1, /device:TPU:1, one launch (start us, length us, event | category | flops | bytes accessed | tf_op | source)
XLA Modules:
  0.0 150.1 jit_solution(16598538469727087379)
XLA Ops:
  0.0 1.1 reshape.10
  1.1 0.4 copy.6
  1.4 0.2 reshape.11.fcp
  1.6 0.0 copy-start
  1.6 1.3 copy-done
  2.9 0.0 copy-start.1
  2.9 0.7 copy-done.1
  3.6 0.0 copy-start.2
  3.6 0.7 copy-done.2
  4.2 0.0 copy-start.3
  4.2 0.7 copy-done.3
  4.9 99.5 %exchange.1 = (bf16[2,8,4,2,128,128]{5,4,3,2,1,0:T(8,128)(2,1)S(1)}, bf16[8,128,256]{2,1,0:T(8,128)(2,1)S(1)}, bf16[8,128,256]{2,1,0:T(8,128)(2,1)S(1)}, bf16[2,128,256]{2,1,0:T(8,128)(2,1)S(1)}) custom-call(s32[4,24]{1,0:T(4,128)S(1)} %copy-done.1, s32[4]{0:T(128)S(1)} %copy-done.2, s32[8]{0:T(128)S(1)} %copy-done.3, bf16[3,128,1536]{2,1,0:T(8,128)(2,1)S(1)} %bitcast.4, ...), custom_call_target="tpu_custom_call" | custom-call | tf_op jit(solution)/shard_map/exchange/pallas_call | solution.py:367
  104.4 45.8 %update.1 = bf16[1024,1024]{1,0:T(8,128)(2,1)} custom-call(s32[4,24]{1,0:T(4,128)S(1)} %copy-done.1, s32[4]{0:T(128)S(1)} %copy-done.2, s32[8]{0:T(128)S(1)} %copy-done.3, bf16[2,8,4,2,128,128]{5,4,3,2,1,0:T(8,128)(2,1)S(1)} %get-tuple-element.9.xr, bf16[8,128,256]{2,1,0:T(8,128)(2,1)S(1)} %get-tuple-element.10.pr, ...), custom_call_target="tpu_custom_call" | custom-call | tf_op jit(solution)/shard_map/update/pallas_call | solution.py:529
Async XLA Ops:
  1.6 1.3 copy-start
  2.9 0.7 copy-start.1
  3.6 0.7 copy-start.2
  4.2 0.7 copy-start.3

commit v2 on v1

--- a/solution.py
+++ b/solution.py
@@ -12,7 +12,8 @@
 BLOCKS = 24
 BF16 = jnp.bfloat16
 F32 = jnp.float32
-LAG = 1
+LAG = 2
+FIRST_BLOCK = 3
 
 
 def copy_to(src, dst, send, recv, **device):
@@ -46,10 +47,84 @@
     return slice(place * BLK, (place + 1) * BLK)
 
 
+def dot(a, b):
+    ah = a.astype(BF16)
+    bh = b.astype(BF16)
+    al = (a - ah.astype(F32)).astype(BF16)
+    bl = (b - bh.astype(F32)).astype(BF16)
+    return product(ah, bh) + (product(ah, bl) + product(al, bh))
+
+
+def product(a, b):
+    return jnp.dot(a, b, preferred_element_type=F32)
+
+
+STEP = 32
+TOGETHER = 8
+
+
+def small_inverse(d):
+    n = d.shape[0]
+    rows = lax.broadcasted_iota(jnp.int32, (n, n), 0)
+    cols = lax.broadcasted_iota(jnp.int32, (n, n), 1)
+    for k in range(0, n, TOGETHER):
+        down = [jnp.broadcast_to(d[:, k + i : k + i + 1], (n, n)) for i in range(TOGETHER)]
+        across = [d[k + i : k + i + 1, :] for i in range(TOGETHER)]
+        for p in range(TOGETHER):
+            at = k + p
+            base = down[p]
+            inv = 1.0 / base[at : at + 1, :]
+            scales = [base[k + i : k + i + 1, :] * inv for i in range(TOGETHER)]
+            scaled = across[p] * inv
+            d = d - base * scaled
+            for i in range(TOGETHER):
+                if i != p:
+                    down[i] = jnp.where(rows == at, scales[i], down[i] - base * scales[i])
+                    across[i] = across[i] - scales[i] * across[p]
+            down[p] = jnp.where(rows == at, -inv, base * inv)
+            across[p] = scaled
+        for i in range(TOGETHER):
+            d = jnp.where(rows == k + i, across[i], d)
+        for i in range(TOGETHER):
+            d = jnp.where(cols == k + i, down[i], d)
+    return -d
+
+
+def sweep_block(a):
+    across = a[0:STEP, :]
+    down = a[:, 0:STEP]
+    inv = small_inverse(a[0:STEP, 0:STEP])
+    q = dot(inv, across)
+    qt = dot(down, inv)
+    a[...] = a[...] - dot(qt, across)
+    a[0:STEP, :] = q
+    a[:, 0:STEP] = qt
+    a[0:STEP, 0:STEP] = -inv
+    n = a.shape[0]
+    a[...] = pltpu.roll(pltpu.roll(a[...], n - STEP, 0), n - STEP, 1)
+
+
+def from_lower(a, co):
+    lower = jnp.concatenate([co[0], co[1]], axis=0).astype(F32)
+    ri = lax.broadcasted_iota(jnp.int32, (PANEL, PANEL), 0)
+    ci = lax.broadcasted_iota(jnp.int32, (PANEL, PANEL), 1)
+    a[...] = lower + jnp.where(ri < ci, lower.T, 0.0)
+
+
+def times_inverse(t, pr, a):
+    m = -a[...]
+    high = m.astype(BF16)
+    low = (m - high.astype(F32)).astype(BF16)
+    for b in range(0, N, 2):
+        rows = pr[b : b + 2].reshape(2 * BLK, PANEL)
+        both = product(rows, high) + product(rows, low)
+        t[b : b + 2] = both.astype(BF16).reshape(2, BLK, PANEL)
+
+
 def exchange_kernel(
     cb, live, fin, contrib, fcp,
-    xr_o, pr_o, pc_o, co_o,
-    px, pxr, pz, pzr, pb, pr, pt, pc, co, zs, zr, xs, xr,
+    xr_o, t_o, pc_o,
+    a, t, px, pxr, pz, pzr, pb, pr, pt, pc, co, zs, zr, xs, xr,
     px_s, px_r, pz_s, pz_r, pr_s, pr_r, t_s, t_r, pc_s, pc_r, co_s, co_r,
     z_s, z_r, x_s, x_r, f_s, f_r, o_s,
 ):
@@ -120,10 +195,13 @@
     def pz_copy(dest, slot):
         return copy_to(pz.at[dest], pzr.at[slot], pz_s.at[dest], pz_r.at[slot], col=dest)
 
-    @pl.loop(1, N)
+    @pl.loop(0, N)
     def _(i):
-        dest = (col + ring_offset(i)) % N
-        pz_copy(dest, col).start()
+        dest = jnp.where(row == 0, i, (col + ring_offset(i)) % N)
+
+        @pl.when(dest != col)
+        def _():
+            pz_copy(dest, col).start()
 
     def z_copies(dest, slot, by, act):
         for k in range(3):
@@ -134,10 +212,15 @@
                     z_s.at[dest], z_r.at[slot], col=dest,
                 ))
 
-    @pl.loop(1, N)
-    def _(i):
-        dest = (col + ring_offset(i)) % N
-        z_copies(dest, col, dest, lambda copy: copy.start())
+    def start_z():
+        @pl.loop(1, N)
+        def _(i):
+            dest = (col + ring_offset(i)) % N
+            z_copies(dest, col, dest, lambda copy: copy.start())
+
+    @pl.when(chip > 0)
+    def _():
+        start_z()
 
     @pl.loop(1, N)
     def _(i):
@@ -149,8 +232,8 @@
         c = fin[j] >> 1
         column = 12 * (fin[j] & 1)
         q = jnp.int32(-1)
-        for a in range(BLOCKS):
-            q = jnp.where(cb[c, a] == N * row + col, a, q)
+        for entry in range(BLOCKS):
+            q = jnp.where(cb[c, entry] == N * row + col, entry, q)
         at = cb[c, column]
         valid = (q >= column) & (q < live[c])
         block = pzr[j, 0:BLK].astype(F32)
@@ -180,41 +263,16 @@
 
     pt_copy = copy_to(pb, pt, t_s, t_r, row=col, col=row)
 
-    @pl.when(row != col)
-    def _():
-        pt_copy.start()
+    def co_copy(dest):
+        return copy_to(pr.at[pl.ds(0, 2)], co, co_s.at[dest], co_r, row=dest)
 
     @pl.loop(1, N)
     def _(i):
         dest = (col + ring_offset(i)) % N
 
-        @pl.when((dest <= row) | (row == 0))
+        @pl.when((dest <= row) | ((row == 0) & (col < 2)))
         def _():
             pr_copy(dest, col).start()
-
-    @pl.when(row == col)
-    def _():
-        pt[...] = pb[...]
-
-    @pl.when(row != col)
-    def _():
-        pt_copy.wait_recv()
-
-    def pc_copy(dest, slot):
-        return copy_to(pt, pc.at[slot], pc_s.at[dest], pc_r.at[slot], row=dest)
-
-    @pl.loop(1, N)
-    def _(i):
-        dest = (row + i) % N
-
-        @pl.when(dest >= col)
-        def _():
-            pc_copy(dest, row).start()
-
-    pc[row] = pt[...]
-
-    def co_copy(dest):
-        return copy_to(pr.at[pl.ds(0, 2)], co, co_s.at[dest], co_r, row=dest)
 
     @pl.when(row == 0)
     def _():
@@ -228,6 +286,36 @@
             co_copy(dest).start()
 
         co[...] = pr[0:2]
+
+    @pl.when(chip == 0)
+    def _():
+        start_z()
+
+    @pl.when(row != col)
+    def _():
+        pt_copy.start()
+
+    @pl.when(row == col)
+    def _():
+        pt[...] = pb[...]
+
+    def pc_copy(dest, slot):
+        return copy_to(pt, pc.at[slot], pc_s.at[dest], pc_r.at[slot], row=dest)
+
+    def pass_on_columns():
+        @pl.when(row != col)
+        def _():
+            pt_copy.wait_recv()
+
+        @pl.loop(1, N)
+        def _(i):
+            dest = (row + i) % N
+
+            @pl.when(dest >= col)
+            def _():
+                pc_copy(dest, row).start()
+
+        pc[row] = pt[...]
 
     needed = chip >= col // 2
 
@@ -278,32 +366,46 @@
 
             f_copy(before, core).start()
 
-    @pl.when(row != 0)
-    def _():
-        co_copy(row).wait_recv()
-
-    @pl.loop(1, N)
-    def _(i):
-        b = (col + i) % N
-
-        @pl.when(((row == 0) & (b > 1)) | ((row > 0) & (col <= row)))
-        def _():
-            pr_copy(b, b).wait_recv()
-
-        @pl.when(row >= col)
-        def _():
+        @pl.when(i == FIRST_BLOCK)
+        def _():
+            @pl.when(row != 0)
+            def _():
+                co_copy(row).wait_recv()
+
+            from_lower(a, co)
+
+        @pl.when((i >= FIRST_BLOCK) & (i < FIRST_BLOCK + 4) & (row >= col))
+        def _():
+            @pl.loop(0, 2)
+            def _(_i):
+                sweep_block(a)
+
+    pass_on_columns()
+
+    @pl.when(row >= col)
+    def _():
+        @pl.loop(1, N)
+        def _(i):
+            b = (col + i) % N
+
+            @pl.when((row > 0) | (b > 1))
+            def _():
+                pr_copy(b, b).wait_recv()
+
+    out_t = pltpu.make_async_copy(t, t_o, o_s.at[0])
+    out_pc = pltpu.make_async_copy(pc, pc_o, o_s.at[1])
+    out_xr = pltpu.make_async_copy(xr, xr_o, o_s.at[2])
+
+    @pl.when(row >= col)
+    def _():
+        times_inverse(t, pr, a)
+        out_t.start()
+
+        @pl.loop(1, N)
+        def _(i):
             slot = (row + i) % N
             pc_copy(slot, slot).wait_recv()
 
-    out_co = pltpu.make_async_copy(co, co_o, o_s.at[0])
-    out_pr = pltpu.make_async_copy(pr, pr_o, o_s.at[1])
-    out_pc = pltpu.make_async_copy(pc, pc_o, o_s.at[2])
-    out_xr = pltpu.make_async_copy(xr, xr_o, o_s.at[3])
-    out_co.start()
-
-    @pl.when(row >= col)
-    def _():
-        out_pr.start()
         out_pc.start()
 
     @pl.when(needed)
@@ -316,10 +418,8 @@
     def _():
         out_xr.start()
         out_xr.wait()
-        out_pr.wait()
+        out_t.wait()
         out_pc.wait()
-
-    out_co.wait()
 
     @pl.loop(1, N)
     def _(i):
@@ -329,7 +429,7 @@
         pz_copy(c, col).wait_send()
         z_copies(c, col, c, lambda copy: copy.wait_send())
 
-        @pl.when((c <= row) | (row == 0))
+        @pl.when((c <= row) | ((row == 0) & (col < 2)))
         def _():
             pr_copy(c, col).wait_send()
 
@@ -370,11 +470,12 @@
             jax.ShapeDtypeStruct((2, N, CHIPS, 2, *block), BF16),
             jax.ShapeDtypeStruct((N, *panel), BF16),
             jax.ShapeDtypeStruct((N, *panel), BF16),
-            jax.ShapeDtypeStruct((2, *panel), BF16),
         ],
         in_specs=[smem, smem, smem, vmem, vmem],
-        out_specs=[any_] * 4,
+        out_specs=[any_] * 3,
         scratch_shapes=[
+            pltpu.VMEM((PANEL, PANEL), F32),
+            pltpu.VMEM((N, *panel), BF16),
             pltpu.VMEM((N, *block), BF16),
             pltpu.VMEM((N, *block), BF16),
             pltpu.VMEM((N, BLK + 32, BLK), BF16),
@@ -397,7 +498,7 @@
             dma((N,)), dma((N,)),
             dma((N, CHIPS)), dma((N, CHIPS)),
             dma((N,)), dma((N,)),
-            dma((4,)),
+            dma((3,)),
         ],
         compiler_params=pltpu.CompilerParams(
             collective_id=0, has_side_effects=True, vmem_limit_bytes=40 << 20
@@ -406,66 +507,13 @@
     )(cb, live, fin, contrib, fcp)
 
 
-def dot(a, b):
-    return jnp.dot(a, b, preferred_element_type=F32, precision=lax.Precision.HIGHEST)
-
-
-def small_inverse(d):
-    n = d.shape[0]
-    rows = lax.broadcasted_iota(jnp.int32, (n, n), 0)
-    cols = lax.broadcasted_iota(jnp.int32, (n, n), 1)
-    for k in range(n):
-        inv = 1.0 / d[k : k + 1, k : k + 1]
-        across = d[k : k + 1, :] * inv
-        down = d[:, k : k + 1]
-        d = d - down * across
-        d = jnp.where(rows == k, across, d)
-        d = jnp.where(cols == k, jnp.where(rows == k, -inv, down * inv), d)
-    return -d
-
-
-STEP = 32
-
-
-def sweep_block(a):
-    across = a[0:STEP, :]
-    down = a[:, 0:STEP]
-    inv = small_inverse(a[0:STEP, 0:STEP])
-    q = dot(inv, across)
-    qt = dot(down, inv)
-    a[...] = a[...] - dot(qt, across)
-    a[0:STEP, :] = q
-    a[:, 0:STEP] = qt
-    a[0:STEP, 0:STEP] = -inv
-    n = a.shape[0]
-    a[...] = pltpu.roll(pltpu.roll(a[...], n - STEP, 0), n - STEP, 1)
-
-
-def update_kernel(cb, live, fin, xr, pr, pc, co, out, a, t, total, rowq, colq, colc, jof):
+def update_kernel(cb, live, fin, xr, t, pc, out, total, rowq, colq, colc, jof):
     row = lax.axis_index("row")
     col = lax.axis_index("col")
     p = pl.program_id(0)
 
     @pl.when((p == 0) & (row >= col))
     def _():
-        lower = jnp.concatenate([co[0], co[1]], axis=0).astype(F32)
-        ri = lax.broadcasted_iota(jnp.int32, (PANEL, PANEL), 0)
-        ci = lax.broadcasted_iota(jnp.int32, (PANEL, PANEL), 1)
-        a[...] = lower + jnp.where(ri < ci, lower.T, 0.0)
-
-        @pl.loop(0, PANEL // STEP)
-        def _(i):
-            sweep_block(a)
-
-        m = -a[...]
-        high = m.astype(BF16)
-        low = (m - high.astype(F32)).astype(BF16)
-        rows = pr[...].reshape(N * BLK, PANEL)
-        t[...] = (
-            jnp.dot(rows, high, preferred_element_type=F32)
-            + jnp.dot(rows, low, preferred_element_type=F32)
-        ).astype(BF16)
-
         for i in range(4 * N):
             rowq[i] = -1
             colq[i] = -1
@@ -495,7 +543,7 @@
 
     @pl.when(row >= col)
     def _():
-        rows = t[pl.ds(pl.multiple_of(p * BLK, BLK), BLK), :]
+        rows = t[p]
         for b in range(0, N, 2):
             columns = pc[b : b + 2].reshape(2 * BLK, PANEL)
             total[:, b * BLK : (b + 2) * BLK] = -lax.dot_general(
@@ -522,7 +570,7 @@
         out[...] = jnp.where(keep, total[...], 0.0).astype(BF16)
 
 
-def update(cb, live, fin, xr, pr, pc, co):
+def update(cb, live, fin, xr, t, pc):
     smem = pl.BlockSpec(memory_space=pltpu.SMEM)
     vmem = pl.BlockSpec(memory_space=pltpu.VMEM)
     ints = lambda n: pltpu.SMEM((n,), jnp.int32)
@@ -530,24 +578,22 @@
         update_kernel,
         grid=(N,),
         out_shape=jax.ShapeDtypeStruct((N * BLK, N * BLK), BF16),
-        in_specs=[smem] * 3 + [vmem] * 4,
+        in_specs=[smem] * 3 + [vmem] * 3,
         out_specs=pl.BlockSpec((BLK, N * BLK), lambda p: (p, 0)),
         scratch_shapes=[
-            pltpu.VMEM((PANEL, PANEL), F32),
-            pltpu.VMEM((N * BLK, PANEL), BF16),
             pltpu.VMEM((BLK, N * BLK), F32),
             ints(4 * N), ints(4 * N), ints(4 * N), ints(N),
         ],
         compiler_params=pltpu.CompilerParams(vmem_limit_bytes=40 << 20),
         name="update",
-    )(cb, live, fin, xr, pr, pc, co)
+    )(cb, live, fin, xr, t, pc)
 
 
 def body(front_cols, contrib, child_blocks, child_live, finish):
     packed = front_cols.reshape(N, 4, 32, 32).transpose(0, 2, 1, 3).reshape(N, 32, BLK)
     pieces = contrib.reshape(3, BLK, 12 * BLK)
-    xr, pr, pc, co = exchange(child_blocks, child_live, finish, pieces, packed)
-    return update(child_blocks, child_live, finish, xr, pr, pc, co)
+    xr, t, pc = exchange(child_blocks, child_live, finish, pieces, packed)
+    return update(child_blocks, child_live, finish, xr, t, pc)
 
 
 def solution(mesh):

time: 150 us -> 109 us (0.73)
  Pallas kernels: 145 us -> 104 us
    pallas_call x1, Pallas kernels: 45.8 us -> 7.03 us  [update(): pl.pallas_call(update_kernel, grid=(N,), out_shape=jax.ShapeDtypeStruct((...]
    pallas_call x1, Pallas kernels: 99.5 us -> 97.3 us  [exchange(): pl.pallas_call(exchange_kernel, out_shape=[jax.ShapeDtypeStruct((2, N, CH...]
where the time goes in v2:
time: 109 us
  Pallas kernels  104 us (95%)
  local copies, waits for them, and re-layouts  4.85 us (4%)
    pallas_call x1, Pallas kernels, exchange(): pl.pallas_call(exchange_kernel, out_shape=[jax.ShapeDtypeStruct((2, N, CH...  97.3 us
    pallas_call x1, Pallas kernels, update(): pl.pallas_call(update_kernel, grid=(N,), out_shape=jax.ShapeDtypeStruct((...  7.03 us
    unnamed x8, local copies, waits for them, and re-layouts  3.26 us

profile of v2, /device:TPU:1, one launch (start us, length us, event | category | flops | bytes accessed | tf_op | source)
XLA Modules:
  0.0 109.2 jit_solution(13144413179326238367)
XLA Ops:
  0.0 1.1 reshape.10
  1.1 0.4 copy.6
  1.4 0.2 reshape.11.fcp
  1.6 0.0 copy-start
  1.6 1.3 %copy-done = bf16[1,384,1536]{2,1,0:T(8,128)(2,1)S(1)} copy-done((bf16[1,384,1536]{2,1,0:T(8,128)(2,1)S(1)}, bf16[1,384,1536]{2,1,0:T(8,128)(2,1)}, u32[]{:S(2)}) %copy-start) | copy-done | bytes 1179672
  2.9 0.0 copy-start.1
  2.9 0.7 copy-done.1
  3.6 0.0 copy-start.2
  3.6 0.7 copy-done.2
  4.2 0.0 copy-start.3
  4.2 0.7 copy-done.3
  4.9 97.3 %exchange.1 = (bf16[2,8,4,2,128,128]{5,4,3,2,1,0:T(8,128)(2,1)S(1)}, bf16[8,128,256]{2,1,0:T(8,128)(2,1)S(1)}, bf16[8,128,256]{2,1,0:T(8,128)(2,1)S(1)}) custom-call(s32[4,24]{1,0:T(4,128)S(1)} %copy-done.1, s32[4]{0:T(128)S(1)} %copy-done.2, s32[8]{0:T(128)S(1)} %copy-done.3, bf16[3,128,1536]{2,1,0:T(8,128)(2,1)S(1)} %bitcast.4, ...), custom_call_target="tpu_custom_call" | custom-call | tf_op jit(solution)/shard_map/exchange/pallas_call | solution.py:467
  102.2 7.0 %update.1 = bf16[1024,1024]{1,0:T(8,128)(2,1)} custom-call(s32[4,24]{1,0:T(4,128)S(1)} %copy-done.1, s32[4]{0:T(128)S(1)} %copy-done.2, s32[8]{0:T(128)S(1)} %copy-done.3, bf16[2,8,4,2,128,128]{5,4,3,2,1,0:T(8,128)(2,1)S(1)} %get-tuple-element.8.xr, bf16[8,128,256]{2,1,0:T(8,128)(2,1)S(1)} %get-tuple-element.9.t, bf16[8,128,256]{2,1,0:T(8,128)(2,1)S(1)} %get-tuple-element.10.pc), custom_call_target="tpu_custom_call" | custom-call | tf_op jit(solution)/shard_map/update/pallas_call | solution.py:577
Async XLA Ops:
  1.6 1.3 %copy-start = (bf16[1,384,1536]{2,1,0:T(8,128)(2,1)S(1)}, bf16[1,384,1536]{2,1,0:T(8,128)(2,1)}, u32[]{:S(2)}) copy-start(bf16[1,384,1536]{2,1,0:T(8,128)(2,1)} %param.6) | copy-start | bytes 3538948
  2.9 0.7 copy-start.1
  3.6 0.7 copy-start.2
  4.2 0.7 copy-start.3

commit v3 on v2

--- a/solution.py
+++ b/solution.py
@@ -13,7 +13,10 @@
 BF16 = jnp.bfloat16
 F32 = jnp.float32
 LAG = 2
-FIRST_BLOCK = 3
+AHEAD = 2
+SUM_STEP = 2
+COLUMNS_STEP = 4
+FIRST_BLOCK = 4
 
 
 def copy_to(src, dst, send, recv, **device):
@@ -31,8 +34,8 @@
     return jnp.where(i % 2 == 1, (i + 1) // 2, (N - i // 2) % N)
 
 
-def first_kept(col):
-    return jnp.where(col < 4, 0, jnp.where(col < 6, 1, 2))
+def first_kept(row, col):
+    return jnp.maximum(col - 1 - (row % 4) // 2, 0) // 2
 
 
 def chosen(cases):
@@ -178,6 +181,23 @@
                 zs[dest, k, c] = chosen([(first == m - c, contrib[k, :, column_block(m)]) for m in ms])
     zr[col] = zs[col]
 
+    def z_copies(dest, slot, by, act):
+        for k in range(3):
+            @pl.when(first_kept(row, by) == k)
+            def _():
+                act(copy_to(
+                    zs.at[dest, pl.ds(k, 3 - k)], zr.at[slot, pl.ds(k, 3 - k)],
+                    z_s.at[dest], z_r.at[slot], col=dest,
+                ))
+
+    def start_z(first, end):
+        @pl.loop(first, end)
+        def _(i):
+            dest = (col + ring_offset(i)) % N
+            z_copies(dest, col, dest, lambda copy: copy.start())
+
+    start_z(1, 1 + AHEAD)
+
     from_row = [jnp.int32(0)] * N
     for q in range(BLOCKS):
         at = cb[child, q] - N * row
@@ -203,101 +223,79 @@
         def _():
             pz_copy(dest, col).start()
 
-    def z_copies(dest, slot, by, act):
-        for k in range(3):
-            @pl.when(first_kept(by) == k)
-            def _():
-                act(copy_to(
-                    zs.at[dest, pl.ds(k, 3 - k)], zr.at[slot, pl.ds(k, 3 - k)],
-                    z_s.at[dest], z_r.at[slot], col=dest,
-                ))
-
-    def start_z():
+    def pr_copy(dest, slot):
+        return copy_to(pb, pr.at[slot], pr_s.at[dest], pr_r.at[slot], col=dest)
+
+    pt_copy = copy_to(pb, pt, t_s, t_r, row=col, col=row)
+
+    def co_copy(dest):
+        return copy_to(pr.at[pl.ds(0, 2)], co, co_s.at[dest], co_r, row=dest)
+
+    def sum_panel():
+        @pl.loop(1, N)
+        def _(i):
+            pz_copy((col + i) % N, (col + i) % N).wait_recv()
+
+        left = jnp.zeros((BLK, BLK), F32)
+        right = jnp.zeros((BLK, BLK), F32)
+        for j in range(N):
+            c = fin[j] >> 1
+            column = 12 * (fin[j] & 1)
+            q = jnp.int32(-1)
+            for entry in range(BLOCKS):
+                q = jnp.where(cb[c, entry] == N * row + col, entry, q)
+            at = cb[c, column]
+            valid = (q >= column) & (q < live[c])
+            block = pzr[j, 0:BLK].astype(F32)
+            left += jnp.where(valid & (at == 0), block, 0.0)
+            right += jnp.where(valid & (at == 1), block, 0.0)
+        lane = lax.broadcasted_iota(jnp.int32, (32, BLK), 1) // 32
+        packed = [pzr[j, BLK:].astype(F32) for j in range(N)]
+        for s in range(4):
+            parts = []
+            for side in range(2):
+                part = jnp.zeros((32, BLK), F32)
+                for j in range(4):
+                    moved = packed[4 * side + j]
+                    if (j - s) % 4:
+                        moved = pltpu.roll(moved, 32 * ((j - s) % 4), 1)
+                    part = jnp.where(lane == j, moved, part)
+                parts.append(part)
+            rows = slice(32 * s, 32 * s + 32)
+            row_ids = (N * row + col) * BLK + 32 * s + lax.broadcasted_iota(jnp.int32, (32, BLK), 0)
+            col_ids = lax.broadcasted_iota(jnp.int32, (32, BLK), 1)
+            pb[rows, 0:BLK] = jnp.where(row_ids >= col_ids, left[rows] + parts[0], 0.0).astype(BF16)
+            pb[rows, BLK:] = jnp.where(row_ids >= col_ids + BLK, right[rows] + parts[1], 0.0).astype(BF16)
+        pr[col] = pb[...]
+
         @pl.loop(1, N)
         def _(i):
             dest = (col + ring_offset(i)) % N
-            z_copies(dest, col, dest, lambda copy: copy.start())
-
-    @pl.when(chip > 0)
-    def _():
-        start_z()
-
-    @pl.loop(1, N)
-    def _(i):
-        pz_copy((col + i) % N, (col + i) % N).wait_recv()
-
-    left = jnp.zeros((BLK, BLK), F32)
-    right = jnp.zeros((BLK, BLK), F32)
-    for j in range(N):
-        c = fin[j] >> 1
-        column = 12 * (fin[j] & 1)
-        q = jnp.int32(-1)
-        for entry in range(BLOCKS):
-            q = jnp.where(cb[c, entry] == N * row + col, entry, q)
-        at = cb[c, column]
-        valid = (q >= column) & (q < live[c])
-        block = pzr[j, 0:BLK].astype(F32)
-        left += jnp.where(valid & (at == 0), block, 0.0)
-        right += jnp.where(valid & (at == 1), block, 0.0)
-    lane = lax.broadcasted_iota(jnp.int32, (32, BLK), 1) // 32
-    packed = [pzr[j, BLK:].astype(F32) for j in range(N)]
-    for s in range(4):
-        parts = []
-        for side in range(2):
-            part = jnp.zeros((32, BLK), F32)
-            for j in range(4):
-                moved = packed[4 * side + j]
-                if (j - s) % 4:
-                    moved = pltpu.roll(moved, 32 * ((j - s) % 4), 1)
-                part = jnp.where(lane == j, moved, part)
-            parts.append(part)
-        rows = slice(32 * s, 32 * s + 32)
-        row_ids = (N * row + col) * BLK + 32 * s + lax.broadcasted_iota(jnp.int32, (32, BLK), 0)
-        col_ids = lax.broadcasted_iota(jnp.int32, (32, BLK), 1)
-        pb[rows, 0:BLK] = jnp.where(row_ids >= col_ids, left[rows] + parts[0], 0.0).astype(BF16)
-        pb[rows, BLK:] = jnp.where(row_ids >= col_ids + BLK, right[rows] + parts[1], 0.0).astype(BF16)
-    pr[col] = pb[...]
-
-    def pr_copy(dest, slot):
-        return copy_to(pb, pr.at[slot], pr_s.at[dest], pr_r.at[slot], col=dest)
-
-    pt_copy = copy_to(pb, pt, t_s, t_r, row=col, col=row)
-
-    def co_copy(dest):
-        return copy_to(pr.at[pl.ds(0, 2)], co, co_s.at[dest], co_r, row=dest)
-
-    @pl.loop(1, N)
-    def _(i):
-        dest = (col + ring_offset(i)) % N
-
-        @pl.when((dest <= row) | ((row == 0) & (col < 2)))
-        def _():
-            pr_copy(dest, col).start()
-
-    @pl.when(row == 0)
-    def _():
-        for b in range(2):
-            @pl.when(col != b)
-            def _():
-                pr_copy(b, b).wait_recv()
-
-        @pl.loop(1, N)
-        def _(dest):
-            co_copy(dest).start()
-
-        co[...] = pr[0:2]
-
-    @pl.when(chip == 0)
-    def _():
-        start_z()
-
-    @pl.when(row != col)
-    def _():
-        pt_copy.start()
-
-    @pl.when(row == col)
-    def _():
-        pt[...] = pb[...]
+
+            @pl.when((dest <= row) | ((row == 0) & (col < 2)))
+            def _():
+                pr_copy(dest, col).start()
+
+        @pl.when(row == 0)
+        def _():
+            for b in range(2):
+                @pl.when(col != b)
+                def _():
+                    pr_copy(b, b).wait_recv()
+
+            @pl.loop(1, N)
+            def _(dest):
+                co_copy(dest).start()
+
+            co[...] = pr[0:2]
+
+        @pl.when(row != col)
+        def _():
+            pt_copy.start()
+
+        @pl.when(row == col)
+        def _():
+            pt[...] = pb[...]
 
     def pc_copy(dest, slot):
         return copy_to(pt, pc.at[slot], pc_s.at[dest], pc_r.at[slot], row=dest)
@@ -334,6 +332,15 @@
             @pl.when(i > 0)
             def _():
                 z_copies(j, j, col, lambda copy: copy.wait_recv())
+                start_z(i + AHEAD, jnp.minimum(i + AHEAD + 1, N))
+
+            @pl.when(i == SUM_STEP)
+            def _():
+                sum_panel()
+
+            @pl.when(i == COLUMNS_STEP)
+            def _():
+                pass_on_columns()
 
             c = fin[j] >> 1
             for dest in range(CHIPS):
@@ -379,8 +386,6 @@
             @pl.loop(0, 2)
             def _(_i):
                 sweep_block(a)
-
-    pass_on_columns()
 
     @pl.when(row >= col)
     def _():

time: 109 us -> 94.7 us (0.87)
  the two profiles are of different devices: /device:TPU:1 before, /device:TPU:71 now
where the time goes in v3:
time: 94.7 us; the launch traced here: 94.4 us
  Pallas kernels  89.5 us (95%)
  local copies, waits for them, and re-layouts  4.85 us (5%)
    pallas_call x1, Pallas kernels, exchange(): pl.pallas_call(exchange_kernel, out_shape=[jax.ShapeDtypeStruct((2, N, CH...  82.5 us
    pallas_call x1, Pallas kernels, update(): pl.pallas_call(update_kernel, grid=(N,), out_shape=jax.ShapeDtypeStruct((...  7.01 us
    unnamed x8, local copies, waits for them, and re-layouts  3.26 us

profile of v3, /device:TPU:71, one launch (start us, length us, event | category | flops | bytes accessed | tf_op | source)
XLA Modules:
  0.0 94.4 jit_solution(7692869911015513359)
XLA Ops:
  0.0 1.1 %reshape.10 = bf16[8,4,32,32]{2,1,0,3:T(4,128)(2,1)S(1)} reshape(bf16[1024,32]{0,1:T(8,128)(2,1)} %param.5) | data formatting | bytes 131072 | tf_op jit(solution)/shard_map/reshape | solution.py:598
  1.1 0.4 copy.6
  1.4 0.2 reshape.11.fcp
  1.6 0.0 copy-start
  1.6 1.3 %copy-done = bf16[1,384,1536]{2,1,0:T(8,128)(2,1)S(1)} copy-done((bf16[1,384,1536]{2,1,0:T(8,128)(2,1)S(1)}, bf16[1,384,1536]{2,1,0:T(8,128)(2,1)}, u32[]{:S(2)}) %copy-start) | copy-done | bytes 1179672
  2.9 0.0 copy-start.1
  2.9 0.7 copy-done.1
  3.6 0.0 copy-start.2
  3.6 0.7 copy-done.2
  4.2 0.0 copy-start.3
  4.2 0.7 copy-done.3
  4.9 82.5 %exchange.1 = (bf16[2,8,4,2,128,128]{5,4,3,2,1,0:T(8,128)(2,1)S(1)}, bf16[8,128,256]{2,1,0:T(8,128)(2,1)S(1)}, bf16[8,128,256]{2,1,0:T(8,128)(2,1)S(1)}) custom-call(s32[4,24]{1,0:T(4,128)S(1)} %copy-done.1, s32[4]{0:T(128)S(1)} %copy-done.2, s32[8]{0:T(128)S(1)} %copy-done.3, bf16[3,128,1536]{2,1,0:T(8,128)(2,1)S(1)} %bitcast.4, ...), custom_call_target="tpu_custom_call" | custom-call | tf_op jit(solution)/shard_map/exchange/pallas_call | solution.py:472
  87.4 7.0 %update.1 = bf16[1024,1024]{1,0:T(8,128)(2,1)} custom-call(s32[4,24]{1,0:T(4,128)S(1)} %copy-done.1, s32[4]{0:T(128)S(1)} %copy-done.2, s32[8]{0:T(128)S(1)} %copy-done.3, bf16[2,8,4,2,128,128]{5,4,3,2,1,0:T(8,128)(2,1)S(1)} %get-tuple-element.8.xr, bf16[8,128,256]{2,1,0:T(8,128)(2,1)S(1)} %get-tuple-element.9.t, bf16[8,128,256]{2,1,0:T(8,128)(2,1)S(1)} %get-tuple-element.10.pc), custom_call_target="tpu_custom_call" | custom-call | tf_op jit(solution)/shard_map/update/pallas_call | solution.py:582
Async XLA Ops:
  1.6 1.3 %copy-start = (bf16[1,384,1536]{2,1,0:T(8,128)(2,1)S(1)}, bf16[1,384,1536]{2,1,0:T(8,128)(2,1)}, u32[]{:S(2)}) copy-start(bf16[1,384,1536]{2,1,0:T(8,128)(2,1)} %param.6) | copy-start | bytes 3538948
  2.9 0.7 copy-start.1
  3.6 0.7 copy-start.2
  4.2 0.7 copy-start.3

commit v4 on v3

--- a/solution.py
+++ b/solution.py
@@ -13,10 +13,12 @@
 BF16 = jnp.bfloat16
 F32 = jnp.float32
 LAG = 2
-AHEAD = 2
-SUM_STEP = 2
-COLUMNS_STEP = 4
+EARLY = 3
+BEFORE_SUM = 5
+SUM_STEP = 3
+COLUMNS_STEP = 5
 FIRST_BLOCK = 4
+RING_STEP = 5
 
 
 def copy_to(src, dst, send, recv, **device):
@@ -126,10 +128,10 @@
 
 def exchange_kernel(
     cb, live, fin, contrib, fcp,
-    xr_o, t_o, pc_o,
-    a, t, px, pxr, pz, pzr, pb, pr, pt, pc, co, zs, zr, xs, xr,
+    xr, t, pc,
+    a, px, pxr, pz, pzr, pb, pr, pt, co, zs, zr, xs,
     px_s, px_r, pz_s, pz_r, pr_s, pr_r, t_s, t_r, pc_s, pc_r, co_s, co_r,
-    z_s, z_r, x_s, x_r, f_s, f_r, o_s,
+    z_s, z_r, x_s, x_r, f_s, f_r,
 ):
     row = lax.axis_index("row")
     col = lax.axis_index("col")
@@ -196,7 +198,7 @@
             dest = (col + ring_offset(i)) % N
             z_copies(dest, col, dest, lambda copy: copy.start())
 
-    start_z(1, 1 + AHEAD)
+    start_z(1, EARLY)
 
     from_row = [jnp.int32(0)] * N
     for q in range(BLOCKS):
@@ -223,6 +225,8 @@
         def _():
             pz_copy(dest, col).start()
 
+    start_z(EARLY, BEFORE_SUM)
+
     def pr_copy(dest, slot):
         return copy_to(pb, pr.at[slot], pr_s.at[dest], pr_r.at[slot], col=dest)
 
@@ -230,6 +234,21 @@
 
     def co_copy(dest):
         return copy_to(pr.at[pl.ds(0, 2)], co, co_s.at[dest], co_r, row=dest)
+
+    def ring_copy(s, right):
+        if right:
+            block, dest = (col + N - s) % N, (col + 1) % N
+        else:
+            block, dest = (col + s) % N, (col + N - 1) % N
+        sem = pr_s.at[s if right else 4 + s]
+        return copy_to(pr.at[block], pr.at[block], sem, pr_r.at[block], col=dest)
+
+    def ring_step(s):
+        for right in (True, False):
+            if s > 0:
+                ring_copy(s, right).wait_recv()
+            if right or s < 3:
+                ring_copy(s, right).start()
 
     def sum_panel():
         @pl.loop(1, N)
@@ -268,13 +287,29 @@
             pb[rows, BLK:] = jnp.where(row_ids >= col_ids + BLK, right[rows] + parts[1], 0.0).astype(BF16)
         pr[col] = pb[...]
 
-        @pl.loop(1, N)
-        def _(i):
-            dest = (col + ring_offset(i)) % N
-
-            @pl.when((dest <= row) | ((row == 0) & (col < 2)))
-            def _():
-                pr_copy(dest, col).start()
+        @pl.when(row == 0)
+        def _():
+            @pl.loop(1, N)
+            def _(i):
+                dest = (col + ring_offset(i)) % N
+
+                @pl.when((dest == 0) | (col < 2))
+                def _():
+                    pr_copy(dest, col).start()
+
+        @pl.when(row > 0)
+        def _():
+            ring_step(0)
+
+        @pl.when(row != col)
+        def _():
+            pt_copy.start()
+
+        @pl.when(row == col)
+        def _():
+            pt[...] = pb[...]
+
+        start_z(BEFORE_SUM, N)
 
         @pl.when(row == 0)
         def _():
@@ -289,14 +324,6 @@
 
             co[...] = pr[0:2]
 
-        @pl.when(row != col)
-        def _():
-            pt_copy.start()
-
-        @pl.when(row == col)
-        def _():
-            pt[...] = pb[...]
-
     def pc_copy(dest, slot):
         return copy_to(pt, pc.at[slot], pc_s.at[dest], pc_r.at[slot], row=dest)
 
@@ -329,18 +356,22 @@
 
         @pl.when(i < N)
         def _():
+            @pl.when(i == SUM_STEP)
+            def _():
+                sum_panel()
+
+            @pl.when(i == COLUMNS_STEP)
+            def _():
+                pass_on_columns()
+
+            for s in range(1, 4):
+                @pl.when((i == RING_STEP + s - 1) & (row > 0))
+                def _():
+                    ring_step(s)
+
             @pl.when(i > 0)
             def _():
                 z_copies(j, j, col, lambda copy: copy.wait_recv())
-                start_z(i + AHEAD, jnp.minimum(i + AHEAD + 1, N))
-
-            @pl.when(i == SUM_STEP)
-            def _():
-                sum_panel()
-
-            @pl.when(i == COLUMNS_STEP)
-            def _():
-                pass_on_columns()
 
             c = fin[j] >> 1
             for dest in range(CHIPS):
@@ -387,44 +418,31 @@
             def _(_i):
                 sweep_block(a)
 
+    @pl.when(row > 0)
+    def _():
+        last = (col + 4) % N
+        pr_copy(last, last).wait_recv()
+
+    @pl.when((row == 0) & (col == 0))
+    def _():
+        @pl.loop(2, N)
+        def _(b):
+            pr_copy(b, b).wait_recv()
+
     @pl.when(row >= col)
     def _():
-        @pl.loop(1, N)
-        def _(i):
-            b = (col + i) % N
-
-            @pl.when((row > 0) | (b > 1))
-            def _():
-                pr_copy(b, b).wait_recv()
-
-    out_t = pltpu.make_async_copy(t, t_o, o_s.at[0])
-    out_pc = pltpu.make_async_copy(pc, pc_o, o_s.at[1])
-    out_xr = pltpu.make_async_copy(xr, xr_o, o_s.at[2])
-
-    @pl.when(row >= col)
-    def _():
         times_inverse(t, pr, a)
-        out_t.start()
 
         @pl.loop(1, N)
         def _(i):
             slot = (row + i) % N
             pc_copy(slot, slot).wait_recv()
 
-        out_pc.start()
-
     @pl.when(needed)
     def _():
         @pl.loop(0, N)
         def _(j):
             f_copy(j, 1 - core).wait_recv()
-
-    @pl.when(row >= col)
-    def _():
-        out_xr.start()
-        out_xr.wait()
-        out_t.wait()
-        out_pc.wait()
 
     @pl.loop(1, N)
     def _(i):
@@ -434,7 +452,7 @@
         pz_copy(c, col).wait_send()
         z_copies(c, col, c, lambda copy: copy.wait_send())
 
-        @pl.when((c <= row) | ((row == 0) & (col < 2)))
+        @pl.when((row == 0) & ((c == 0) | (col < 2)))
         def _():
             pr_copy(c, col).wait_send()
 
@@ -445,6 +463,13 @@
         @pl.when(row == 0)
         def _():
             co_copy(r).wait_send()
+
+    @pl.when(row > 0)
+    def _():
+        for s in range(4):
+            ring_copy(s, True).wait_send()
+            if s < 3:
+                ring_copy(s, False).wait_send()
 
     @pl.when(row != col)
     def _():
@@ -464,7 +489,6 @@
 
 def exchange(cb, live, fin, contrib, fcp):
     dma = pltpu.SemaphoreType.DMA
-    any_ = pl.BlockSpec(memory_space=pl.ANY)
     vmem = pl.BlockSpec(memory_space=pltpu.VMEM)
     smem = pl.BlockSpec(memory_space=pltpu.SMEM)
     block = (BLK, BLK)
@@ -477,10 +501,9 @@
             jax.ShapeDtypeStruct((N, *panel), BF16),
         ],
         in_specs=[smem, smem, smem, vmem, vmem],
-        out_specs=[any_] * 3,
+        out_specs=[vmem] * 3,
         scratch_shapes=[
             pltpu.VMEM((PANEL, PANEL), F32),
-            pltpu.VMEM((N, *panel), BF16),
             pltpu.VMEM((N, *block), BF16),
             pltpu.VMEM((N, *block), BF16),
             pltpu.VMEM((N, BLK + 32, BLK), BF16),
@@ -488,12 +511,10 @@
             pltpu.VMEM(panel, BF16),
             pltpu.VMEM((N, *panel), BF16),
             pltpu.VMEM(panel, BF16),
-            pltpu.VMEM((N, *panel), BF16),
             pltpu.VMEM((2, *panel), BF16),
             pltpu.VMEM((N, 3, 2, *block), BF16),
             pltpu.VMEM((N, 3, 2, *block), BF16),
             pltpu.VMEM((N, 2, 2, *block), BF16),
-            pltpu.VMEM((2, N, CHIPS, 2, *block), BF16),
             dma((N,)), dma((N,)),
             dma((N,)), dma((N,)),
             dma((N,)), dma((N,)),
@@ -503,7 +524,6 @@
             dma((N,)), dma((N,)),
             dma((N, CHIPS)), dma((N, CHIPS)),
             dma((N,)), dma((N,)),
-            dma((3,)),
         ],
         compiler_params=pltpu.CompilerParams(
             collective_id=0, has_side_effects=True, vmem_limit_bytes=40 << 20
@@ -512,12 +532,15 @@
     )(cb, live, fin, contrib, fcp)
 
 
-def update_kernel(cb, live, fin, xr, t, pc, out, total, rowq, colq, colc, jof):
+def update_kernel(cb, live, fin, xr, t, pc, out, total, strip, rowq, colq, colc, jof, sem):
     row = lax.axis_index("row")
     col = lax.axis_index("col")
-    p = pl.program_id(0)
-
-    @pl.when((p == 0) & (row >= col))
+
+    def strip_copy(p):
+        rows = pl.ds(pl.multiple_of(p * BLK, BLK), BLK)
+        return pltpu.make_async_copy(strip.at[p % 2], out.at[rows], sem.at[p % 2])
+
+    @pl.when(row >= col)
     def _():
         for i in range(4 * N):
             rowq[i] = -1
@@ -542,12 +565,7 @@
                     else:
                         colc[N * c + (v & 7)] = jnp.where(cb[c, before] >> 3 == col, 1, 0)
 
-    @pl.when(row < col)
-    def _():
-        out[...] = jnp.zeros_like(out)
-
-    @pl.when(row >= col)
-    def _():
+    def one_strip(p):
         rows = t[p]
         for b in range(0, N, 2):
             columns = pc[b : b + 2].reshape(2 * BLK, PANEL)
@@ -572,7 +590,26 @@
         ri = (N * row + p) * BLK + lax.broadcasted_iota(jnp.int32, (BLK, N * BLK), 0)
         ci = N * BLK * col + lax.broadcasted_iota(jnp.int32, (BLK, N * BLK), 1)
         keep = (ri >= ci) & (ri >= PANEL) & (ci >= PANEL)
-        out[...] = jnp.where(keep, total[...], 0.0).astype(BF16)
+        strip[p % 2] = jnp.where(keep, total[...], 0.0).astype(BF16)
+
+    @pl.when(row < col)
+    def _():
+        strip[...] = jnp.zeros_like(strip)
+
+    @pl.loop(0, N)
+    def _(p):
+        @pl.when(p >= 2)
+        def _():
+            strip_copy(p - 2).wait()
+
+        @pl.when(row >= col)
+        def _():
+            one_strip(p)
+
+        strip_copy(p).start()
+
+    for p in range(N - 2, N):
+        strip_copy(p).wait()
 
 
 def update(cb, live, fin, xr, t, pc):
@@ -581,13 +618,14 @@
     ints = lambda n: pltpu.SMEM((n,), jnp.int32)
     return pl.pallas_call(
         update_kernel,
-        grid=(N,),
         out_shape=jax.ShapeDtypeStruct((N * BLK, N * BLK), BF16),
         in_specs=[smem] * 3 + [vmem] * 3,
-        out_specs=pl.BlockSpec((BLK, N * BLK), lambda p: (p, 0)),
+        out_specs=pl.BlockSpec(memory_space=pl.ANY),
         scratch_shapes=[
             pltpu.VMEM((BLK, N * BLK), F32),
+            pltpu.VMEM((2, BLK, N * BLK), BF16),
             ints(4 * N), ints(4 * N), ints(4 * N), ints(N),
+            pltpu.SemaphoreType.DMA((2,)),
         ],
         compiler_params=pltpu.CompilerParams(vmem_limit_bytes=40 << 20),
         name="update",

time: 94.7 us -> 88.7 us (0.937)
  the two profiles are of different devices: /device:TPU:71 before, /device:TPU:1 now
where the time goes in v4:
time: 88.7 us; the launch traced here: 87.9 us
  Pallas kernels  83 us (94%)
  local copies, waits for them, and re-layouts  4.85 us (5%)
    pallas_call x1, Pallas kernels, exchange(): pl.pallas_call(exchange_kernel, out_shape=[jax.ShapeDtypeStruct((2, N, CH...  76.4 us
    pallas_call x1, Pallas kernels, update(): pl.pallas_call(update_kernel, out_shape=jax.ShapeDtypeStruct((N * BLK, N...  6.6 us
    unnamed x8, local copies, waits for them, and re-layouts  3.26 us

profile of v4, /device:TPU:1, one launch (start us, length us, event | category | flops | bytes accessed | tf_op | source)
XLA Modules:
  0.0 87.9 jit_solution(2160457574375586833)
XLA Ops:
  0.0 1.1 %reshape.10 = bf16[8,4,32,32]{2,1,0,3:T(4,128)(2,1)S(1)} reshape(bf16[1024,32]{0,1:T(8,128)(2,1)} %param.5) | data formatting | bytes 131072 | tf_op jit(solution)/shard_map/reshape | solution.py:636
  1.1 0.4 copy.6
  1.4 0.2 reshape.11.fcp
  1.6 0.0 copy-start
  1.6 1.3 %copy-done = bf16[1,384,1536]{2,1,0:T(8,128)(2,1)S(1)} copy-done((bf16[1,384,1536]{2,1,0:T(8,128)(2,1)S(1)}, bf16[1,384,1536]{2,1,0:T(8,128)(2,1)}, u32[]{:S(2)}) %copy-start) | copy-done | bytes 1179672
  2.9 0.0 copy-start.1
  2.9 0.7 copy-done.1
  3.6 0.0 copy-start.2
  3.6 0.7 copy-done.2
  4.2 0.0 copy-start.3
  4.2 0.7 copy-done.3
  4.9 76.4 %exchange.1 = (bf16[2,8,4,2,128,128]{5,4,3,2,1,0:T(8,128)(2,1)S(1)}, bf16[8,128,256]{2,1,0:T(8,128)(2,1)S(1)}, bf16[8,128,256]{2,1,0:T(8,128)(2,1)S(1)}) custom-call(s32[4,24]{1,0:T(4,128)S(1)} %copy-done.1, s32[4]{0:T(128)S(1)} %copy-done.2, s32[8]{0:T(128)S(1)} %copy-done.3, bf16[3,128,1536]{2,1,0:T(8,128)(2,1)S(1)} %bitcast.4, ...), custom_call_target="tpu_custom_call" | custom-call | tf_op jit(solution)/shard_map/exchange/pallas_call | solution.py:496
  81.3 6.6 %update.1 = bf16[1024,1024]{1,0:T(8,128)(2,1)} custom-call(s32[4,24]{1,0:T(4,128)S(1)} %copy-done.1, s32[4]{0:T(128)S(1)} %copy-done.2, s32[8]{0:T(128)S(1)} %copy-done.3, bf16[2,8,4,2,128,128]{5,4,3,2,1,0:T(8,128)(2,1)S(1)} %get-tuple-element.8.xr, bf16[8,128,256]{2,1,0:T(8,128)(2,1)S(1)} %get-tuple-element.9.t, bf16[8,128,256]{2,1,0:T(8,128)(2,1)S(1)} %get-tuple-element.10.pc), custom_call_target="tpu_custom_call" | custom-call | tf_op jit(solution)/shard_map/update/pallas_call | solution.py:619
Async XLA Ops:
  1.6 1.3 %copy-start = (bf16[1,384,1536]{2,1,0:T(8,128)(2,1)S(1)}, bf16[1,384,1536]{2,1,0:T(8,128)(2,1)}, u32[]{:S(2)}) copy-start(bf16[1,384,1536]{2,1,0:T(8,128)(2,1)} %param.6) | copy-start | bytes 3538948
  2.9 0.7 copy-start.1
  3.6 0.7 copy-start.2
  4.2 0.7 copy-start.3

commit v5 on v4

--- a/solution.py
+++ b/solution.py
@@ -127,7 +127,7 @@
 
 
 def exchange_kernel(
-    cb, live, fin, contrib, fcp,
+    cb, live, fin, contrib, fct,
     xr, t, pc,
     a, px, pxr, pz, pzr, pb, pr, pt, co, zs, zr, xs,
     px_s, px_r, pz_s, pz_r, pr_s, pr_r, t_s, t_r, pc_s, pc_r, co_s, co_r,
@@ -211,7 +211,7 @@
 
     for b in range(N):
         pz[b, 0:BLK] = chosen([(from_row[b] == r, pxr[r]) for r in range(N)])
-        pz[b, BLK:] = fcp[b]
+        pz[b, BLK:] = fct[:, b * BLK : (b + 1) * BLK]
     pzr[col] = pz[col]
 
     def pz_copy(dest, slot):
@@ -268,23 +268,11 @@
             block = pzr[j, 0:BLK].astype(F32)
             left += jnp.where(valid & (at == 0), block, 0.0)
             right += jnp.where(valid & (at == 1), block, 0.0)
-        lane = lax.broadcasted_iota(jnp.int32, (32, BLK), 1) // 32
-        packed = [pzr[j, BLK:].astype(F32) for j in range(N)]
-        for s in range(4):
-            parts = []
-            for side in range(2):
-                part = jnp.zeros((32, BLK), F32)
-                for j in range(4):
-                    moved = packed[4 * side + j]
-                    if (j - s) % 4:
-                        moved = pltpu.roll(moved, 32 * ((j - s) % 4), 1)
-                    part = jnp.where(lane == j, moved, part)
-                parts.append(part)
-            rows = slice(32 * s, 32 * s + 32)
-            row_ids = (N * row + col) * BLK + 32 * s + lax.broadcasted_iota(jnp.int32, (32, BLK), 0)
-            col_ids = lax.broadcasted_iota(jnp.int32, (32, BLK), 1)
-            pb[rows, 0:BLK] = jnp.where(row_ids >= col_ids, left[rows] + parts[0], 0.0).astype(BF16)
-            pb[rows, BLK:] = jnp.where(row_ids >= col_ids + BLK, right[rows] + parts[1], 0.0).astype(BF16)
+        initial = jnp.concatenate([pzr[j, BLK:] for j in range(N)], axis=0).astype(F32).T
+        row_ids = (N * row + col) * BLK + lax.broadcasted_iota(jnp.int32, (BLK, PANEL), 0)
+        col_ids = lax.broadcasted_iota(jnp.int32, (BLK, PANEL), 1)
+        total = jnp.concatenate([left, right], axis=1) + initial
+        pb[...] = jnp.where(row_ids >= col_ids, total, 0.0).astype(BF16)
         pr[col] = pb[...]
 
         @pl.when(row == 0)
@@ -487,7 +475,7 @@
             f_copy(j, core).wait_send()
 
 
-def exchange(cb, live, fin, contrib, fcp):
+def exchange(cb, live, fin, contrib, fct):
     dma = pltpu.SemaphoreType.DMA
     vmem = pl.BlockSpec(memory_space=pltpu.VMEM)
     smem = pl.BlockSpec(memory_space=pltpu.SMEM)
@@ -529,7 +517,7 @@
             collective_id=0, has_side_effects=True, vmem_limit_bytes=40 << 20
         ),
         name="exchange",
-    )(cb, live, fin, contrib, fcp)
+    )(cb, live, fin, contrib, fct)
 
 
 def update_kernel(cb, live, fin, xr, t, pc, out, total, strip, rowq, colq, colc, jof, sem):
@@ -633,9 +621,8 @@
 
 
 def body(front_cols, contrib, child_blocks, child_live, finish):
-    packed = front_cols.reshape(N, 4, 32, 32).transpose(0, 2, 1, 3).reshape(N, 32, BLK)
     pieces = contrib.reshape(3, BLK, 12 * BLK)
-    xr, t, pc = exchange(child_blocks, child_live, finish, pieces, packed)
+    xr, t, pc = exchange(child_blocks, child_live, finish, pieces, front_cols.T)
     return update(child_blocks, child_live, finish, xr, t, pc)
 
 

time: 88.7 us -> 87.9 us (level)
    reshape x3 -> x0, local copies, waits for them, and re-layouts: 1.59 us -> none  [body(): front_cols.reshape(N, 4, 32, 32).transpose(0, 2, 1, 3).reshape(N, 32, BLK)]
    unnamed x8 -> x10, local copies, waits for them, and re-layouts: 3.26 us -> 4.1 us
where the time goes in v5:
time: 87.9 us; the launch traced here: 87.3 us
  Pallas kernels  83.1 us (95%)
  local copies, waits for them, and re-layouts  4.1 us (5%)
    pallas_call x1, Pallas kernels, exchange(): pl.pallas_call(exchange_kernel, out_shape=[jax.ShapeDtypeStruct((2, N, CH...  76.4 us
    pallas_call x1, Pallas kernels, update(): pl.pallas_call(update_kernel, out_shape=jax.ShapeDtypeStruct((N * BLK, N...  6.76 us
    unnamed x10, local copies, waits for them, and re-layouts  4.1 us

profile of v5, /device:TPU:1, one launch (start us, length us, event | category | flops | bytes accessed | tf_op | source)
XLA Modules:
  0.0 87.3 jit_solution(15538654111742870146)
XLA Ops:
  0.0 0.0 copy-start
  0.0 1.3 %copy-done = bf16[1,384,1536]{2,1,0:T(8,128)(2,1)S(1)} copy-done((bf16[1,384,1536]{2,1,0:T(8,128)(2,1)S(1)}, bf16[1,384,1536]{2,1,0:T(8,128)(2,1)}, u32[]{:S(2)}) %copy-start) | copy-done | bytes 1179672
  1.3 0.0 copy-start.1
  1.3 0.8 copy-done.1
  2.1 0.0 copy-start.2
  2.1 0.7 copy-done.2
  2.8 0.0 copy-start.3
  2.8 0.7 copy-done.3
  3.4 0.0 copy-start.4
  3.5 0.7 copy-done.4
  4.1 76.4 %exchange.1 = (bf16[2,8,4,2,128,128]{5,4,3,2,1,0:T(8,128)(2,1)S(1)}, bf16[8,128,256]{2,1,0:T(8,128)(2,1)S(1)}, bf16[8,128,256]{2,1,0:T(8,128)(2,1)S(1)}) custom-call(s32[4,24]{1,0:T(4,128)S(1)} %copy-done.2, s32[4]{0:T(128)S(1)} %copy-done.3, s32[8]{0:T(128)S(1)} %copy-done.4, bf16[3,128,1536]{2,1,0:T(8,128)(2,1)S(1)} %bitcast.2, bf16[32,1024]{1,0:T(8,128)(2,1)S(1)} %bitcast.3), custom_call_target="tpu_custom_call" | custom-call | tf_op jit(solution)/shard_map/exchange/pallas_call | solution.py:484
  80.5 6.8 %update.1 = bf16[1024,1024]{1,0:T(8,128)(2,1)} custom-call(s32[4,24]{1,0:T(4,128)S(1)} %copy-done.2, s32[4]{0:T(128)S(1)} %copy-done.3, s32[8]{0:T(128)S(1)} %copy-done.4, bf16[2,8,4,2,128,128]{5,4,3,2,1,0:T(8,128)(2,1)S(1)} %get-tuple-element.8.xr, bf16[8,128,256]{2,1,0:T(8,128)(2,1)S(1)} %get-tuple-element.9.t, bf16[8,128,256]{2,1,0:T(8,128)(2,1)S(1)} %get-tuple-element.10.pc), custom_call_target="tpu_custom_call" | custom-call | tf_op jit(solution)/shard_map/update/pallas_call | solution.py:607
Async XLA Ops:
  0.0 1.3 %copy-start = (bf16[1,384,1536]{2,1,0:T(8,128)(2,1)S(1)}, bf16[1,384,1536]{2,1,0:T(8,128)(2,1)}, u32[]{:S(2)}) copy-start(bf16[1,384,1536]{2,1,0:T(8,128)(2,1)} %param.6) | copy-start | bytes 3538948
  1.3 0.8 copy-start.1
  2.1 0.7 copy-start.2
  2.8 0.7 copy-start.3
  3.4 0.7 copy-start.4

commit v6 on v5

--- a/solution.py
+++ b/solution.py
@@ -12,7 +12,7 @@
 BLOCKS = 24
 BF16 = jnp.bfloat16
 F32 = jnp.float32
-LAG = 2
+LAG = 3
 EARLY = 3
 BEFORE_SUM = 5
 SUM_STEP = 3

time: 87.9 us -> 88.1 us (level)
  no operation moved by 1% of the time
where the time goes in v6:
time: 88.1 us; the launch traced here: 87.3 us
  Pallas kernels  83.2 us (94%)
  local copies, waits for them, and re-layouts  4.1 us (5%)
    pallas_call x1, Pallas kernels, exchange(): pl.pallas_call(exchange_kernel, out_shape=[jax.ShapeDtypeStruct((2, N, CH...  76.4 us
    pallas_call x1, Pallas kernels, update(): pl.pallas_call(update_kernel, out_shape=jax.ShapeDtypeStruct((N * BLK, N...  6.79 us
    unnamed x10, local copies, waits for them, and re-layouts  4.1 us

profile of v6, /device:TPU:1, one launch (start us, length us, event | category | flops | bytes accessed | tf_op | source)
XLA Modules:
  0.0 87.3 jit_solution(18118633091022070687)
XLA Ops:
  0.0 0.0 copy-start
  0.0 1.3 %copy-done = bf16[1,384,1536]{2,1,0:T(8,128)(2,1)S(1)} copy-done((bf16[1,384,1536]{2,1,0:T(8,128)(2,1)S(1)}, bf16[1,384,1536]{2,1,0:T(8,128)(2,1)}, u32[]{:S(2)}) %copy-start) | copy-done | bytes 1179672
  1.3 0.0 copy-start.1
  1.3 0.8 copy-done.1
  2.1 0.0 copy-start.2
  2.1 0.7 copy-done.2
  2.8 0.0 copy-start.3
  2.8 0.7 copy-done.3
  3.4 0.0 copy-start.4
  3.5 0.7 copy-done.4
  4.1 76.4 %exchange.1 = (bf16[2,8,4,2,128,128]{5,4,3,2,1,0:T(8,128)(2,1)S(1)}, bf16[8,128,256]{2,1,0:T(8,128)(2,1)S(1)}, bf16[8,128,256]{2,1,0:T(8,128)(2,1)S(1)}) custom-call(s32[4,24]{1,0:T(4,128)S(1)} %copy-done.2, s32[4]{0:T(128)S(1)} %copy-done.3, s32[8]{0:T(128)S(1)} %copy-done.4, bf16[3,128,1536]{2,1,0:T(8,128)(2,1)S(1)} %bitcast.2, bf16[32,1024]{1,0:T(8,128)(2,1)S(1)} %bitcast.3), custom_call_target="tpu_custom_call" | custom-call | tf_op jit(solution)/shard_map/exchange/pallas_call | solution.py:484
  80.5 6.8 %update.1 = bf16[1024,1024]{1,0:T(8,128)(2,1)} custom-call(s32[4,24]{1,0:T(4,128)S(1)} %copy-done.2, s32[4]{0:T(128)S(1)} %copy-done.3, s32[8]{0:T(128)S(1)} %copy-done.4, bf16[2,8,4,2,128,128]{5,4,3,2,1,0:T(8,128)(2,1)S(1)} %get-tuple-element.8.xr, bf16[8,128,256]{2,1,0:T(8,128)(2,1)S(1)} %get-tuple-element.9.t, bf16[8,128,256]{2,1,0:T(8,128)(2,1)S(1)} %get-tuple-element.10.pc), custom_call_target="tpu_custom_call" | custom-call | tf_op jit(solution)/shard_map/update/pallas_call | solution.py:607
Async XLA Ops:
  0.0 1.3 %copy-start = (bf16[1,384,1536]{2,1,0:T(8,128)(2,1)S(1)}, bf16[1,384,1536]{2,1,0:T(8,128)(2,1)}, u32[]{:S(2)}) copy-start(bf16[1,384,1536]{2,1,0:T(8,128)(2,1)} %param.6) | copy-start | bytes 3538948
  1.3 0.8 copy-start.1
  2.1 0.7 copy-start.2
  2.8 0.7 copy-start.3
  3.4 0.7 copy-start.4
